TPU v7x, 32 devices: a whole 2x2x4 slice. The times are simulated.
32 devices in a mesh: parts: 2 (over y), db: 4 (over z), loop: 4 (over x, core).
Axes of the slice: x: 2, y: 2, z: 4, core: 2. Of those that a mesh axis runs over, the one named last changes fastest.
Arguments:
- queries: bfloat16 [1024, 1024], P(('parts', 'db')), parts along dimension 0, may hold values from -6 to 6
- database: bfloat16 [65536, 1024], P(('parts', 'db', 'loop')), parts along dimension 0, may hold values from -6 to 6
- pair_query: int32 [32, 32], P(('parts', 'db', 'loop')), parts along dimension 0, may hold values from 0 to 3, as said below
- pair_db: int32 [32, 32], P(('parts', 'db', 'loop')), parts along dimension 0, may hold values from 0 to 15, as said below
- pair_count: int32 [32], P(('parts', 'db', 'loop')), parts along dimension 0, may hold values from 16 to 32, as said below
Outputs:
- new_profiles: float32 [1024, 1024], P(('parts', 'db'), 'loop'), parts along dimension 0
There are 2 independent parts, one for each index of `parts`. A program takes and returns all parts, laid end to end along the dimension named above; each array names one. Nothing has to cross between parts.
Inputs may be any that keep to these rules, and one draw needn't show every extreme that they name: `pair_query`: together with pair_db, each row lists 32 distinct pairs of one of the 4 query blocks and one of the 16 database blocks, a subset and order drawn per shard. `pair_db`: see pair_query. Slots at or after pair_count[g] are unused; the count is 32 on some shard and 16 on another in every draw.
All inputs are finite; a program needn't handle non-finite values.
Results may differ from a plain program's by a relative error of at most 0.00082.
Values may be sent and summed in bfloat16 or wider, within the bound.
No kernel may reach another device: no remote copies, remote signals or barrier semaphores. Data moves between devices by JAX's collectives and lax.ppermute only.
A program may use at most 64 MiB of HBM per device.

v0:
```python
import math

import jax
import jax.numpy as jnp
from jax import lax
from jax.sharding import PartitionSpec as P

BLK = 128


score_gain = 2.0


def per_device(queries, database, pair_query, pair_db, pair_count):
    panels = lax.all_gather(queries, "db", axis=0, tiled=True)
    query_rows, feature_count = panels.shape
    score_scale = score_gain / math.sqrt(feature_count)
    block_rows = BLK
    slot_query = pair_query[0]
    slot_db = pair_db[0]
    live_count = pair_count[0]
    turns = (live_count + 3) // 4

    def visit(turn_no, state_pair):
        summed, totals = state_pair
        first = turn_no * 4
        for offset in range(4):
            slot_no = first + offset
            query_start = slot_query[slot_no] * block_rows
            db_start = slot_db[slot_no] * block_rows
            living = (slot_no < live_count).astype(jnp.float32)
            query_tile = lax.dynamic_slice_in_dim(panels, query_start, block_rows, 0)
            db_tile = lax.dynamic_slice_in_dim(database, db_start, block_rows, 0)
            scores = (
                lax.dot_general(
                    query_tile,
                    db_tile,
                    (((1,), (1,)), ((), ())),
                    preferred_element_type=jnp.float32,
                )
                * score_scale
            )
            weights = jax.nn.sigmoid(scores) * living
            contrib = jnp.dot(
                weights.astype(jnp.bfloat16), db_tile, preferred_element_type=jnp.float32
            )
            old_rows = lax.dynamic_slice_in_dim(summed, query_start, block_rows, 0)
            summed = lax.dynamic_update_slice_in_dim(summed, old_rows + contrib, query_start, 0)
            old_totals = lax.dynamic_slice_in_dim(totals, query_start, block_rows, 0)
            totals = lax.dynamic_update_slice_in_dim(
                totals, old_totals + jnp.sum(weights, axis=1, keepdims=True), query_start, 0
            )
        return (summed, totals)

    start = (
        jnp.zeros((query_rows, feature_count), jnp.float32),
        jnp.zeros((query_rows, 1), jnp.float32),
    )
    summed_rows, total_rows = lax.fori_loop(0, turns, visit, start)
    column_width = feature_count // lax.axis_size("loop")
    own_profiles = lax.dynamic_slice_in_dim(
        queries, lax.axis_index("loop") * column_width, column_width, 1
    ).astype(jnp.float32)
    row_sums, row_weights = (
        lax.psum_scatter(summed_rows, "db", scatter_dimension=0, tiled=True),
        lax.psum_scatter(total_rows, "db", scatter_dimension=0, tiled=True),
    )
    partial_out = lax.psum_scatter(row_sums, "loop", scatter_dimension=1, tiled=True)
    weight_out = lax.psum(row_weights, "loop")
    return own_profiles + partial_out * lax.rsqrt(1.0 + weight_out)


def solution(mesh):
    return jax.shard_map(
        per_device,
        mesh=mesh,
        in_specs=(
            P(("parts", "db"), None),
            P(("parts", "db", "loop"), None),
            P(("parts", "db", "loop"), None),
            P(("parts", "db", "loop"), None),
            P(("parts", "db", "loop")),
        ),
        out_specs=P(("parts", "db"), "loop"),
        check_vma=False,
    )
```

profile of v0, /device:TPU:1, one launch (start us, length us, event | category | flops | bytes accessed | tf_op | source)
XLA Modules:
  0.0 288.8 jit_solution(11570505454245826248)
XLA Ops:
  8.0 30.9 %all-gather.2.cloned.1.call-done = bf16[512,1024]{1,0:T(8,128)(2,1)} async-done(((bf16[128,1024]{1,0:T(8,128)(2,1)}), bf16[512,1024]{1,0:T(8,128)(2,1)}) %all-gather.2.cloned.1.call-update) | async-done | bytes 1048592 | tf_op jit(solution)/shard_map/all_gather | solution.py:15
  39.1 134.2 %while.14 = (s32[]{:T(128)}, f32[512,1024]{1,0:T(8,128)S(1)}, f32[512,1]{0,1:T(1,128)S(1)}, s32[]{:T(128)}, s32[32]{0:T(128)}, /*index=5*/bf16[512,1024]{1,0:T(8...) while((s32[]{:T(128)}, f32[512,1024]{1,0:T(8,128)S(1)}, ...), condition=%wide.region_5.6_spmd, body=%wide.region_0.5_spmd.sunk | while | flops 269418528 | bytes 11805673 | solution.py:59
  39.2 1.5 fusion.87
  42.6 1.3 fusion.88
  47.1 1.3 fusion.90
  55.7 1.2 fusion.94
  58.3 1.5 fusion.87
  61.8 1.3 fusion.88
  66.2 1.3 fusion.90
  74.9 1.2 fusion.94
  77.5 1.5 fusion.87
  80.9 1.3 fusion.88
  85.4 1.3 fusion.90
  96.6 1.5 fusion.87
  100.1 1.3 fusion.88
  104.6 1.3 fusion.90
  113.2 1.2 fusion.94
  115.8 1.5 fusion.87
  119.3 1.3 fusion.88
  123.7 1.3 fusion.90
  135.0 1.5 fusion.87
  138.4 1.3 fusion.88
  142.9 1.3 fusion.90
  154.1 1.5 fusion.87
  157.6 1.3 fusion.88
  162.1 1.3 fusion.90
  173.3 1.3 copy-done
  175.6 61.2 %reduce-scatter.6.cloned.1.call-done = f32[128,1024]{1,0:T(8,128)} async-done(((f32[512,1024]{1,0:T(8,128)}), f32[128,1024]{1,0:T(8,128)}) %reduce-scatter.6.cloned.1.call-update) | async-done | bytes 524304 | tf_op jit(solution)/shard_map/reduce_scatter | solution.py:65
  236.9 19.9 %reduce-scatter.10.cloned.1.call-done = f32[128,1]{1,0:T(8,128)} async-done(((f32[512,1]{1,0:T(8,128)}), f32[128,1]{1,0:T(8,128)}) %reduce-scatter.10.cloned.1.call-update) | async-done | bytes 528
  257.7 7.3 %psum.7 = f32[128,1]{0,1:T(1,128)S(1)} all-reduce(f32[128,1]{0,1:T(1,128)S(1)} %copy.7), channel_id=1, replica_groups=mesh['parts'=2,'db'=4,'loop'=4] {'loop'}, use_global_device_ids=true, to_apply=%region_9.10 | all-reduce | flops 128 | bytes 1024 | tf_op jit(solution)/shard_map/psum | solution.py:69
  265.0 15.6 %reduce-scatter.8.cloned.1.call-done = f32[128,256]{1,0:T(8,128)} async-done(((f32[128,1024]{1,0:T(8,128)}), f32[128,256]{1,0:T(8,128)}) %reduce-scatter.8.cloned.1.call-update) | async-done | bytes 131088 | tf_op jit(solution)/shard_map/reduce_scatter | solution.py:68
  280.7 1.6 multiply_add_fusion
  (95 shorter events, 50.6 us)
Async XLA Ops:
  6.5 32.3 %all-gather.2.cloned.1.call-start = ((), (), s32[]{:S(2)}) async-start(), calls=%async_computation.3 | async-start | bytes 1310720 | tf_op jit(solution)/shard_map/all_gather | solution.py:15
  7.3 229.6 %reduce-scatter.6.cloned.1.call-start = ((), (), s32[]{:S(2)}) async-start(), calls=%async_computation.4 | async-start | bytes 2621440 | tf_op jit(solution)/shard_map/reduce_scatter | solution.py:65
  39.1 12.3 %copy-start.1 = (bf16[512,1024]{1,0:T(8,128)(2,1)S(1)}, bf16[512,1024]{1,0:T(8,128)(2,1)}, u32[]{:S(2)}) copy-start(bf16[512,1024]{1,0:T(8,128)(2,1)} %get-tuple-element.307) | copy-start | bytes 3145732 | tf_op jit(solution)/shard_map/while
  58.3 12.3 %copy-start.1 = (bf16[512,1024]{1,0:T(8,128)(2,1)S(1)}, bf16[512,1024]{1,0:T(8,128)(2,1)}, u32[]{:S(2)}) copy-start(bf16[512,1024]{1,0:T(8,128)(2,1)} %get-tuple-element.307) | copy-start | bytes 3145732 | tf_op jit(solution)/shard_map/while
  77.4 12.3 %copy-start.1 = (bf16[512,1024]{1,0:T(8,128)(2,1)S(1)}, bf16[512,1024]{1,0:T(8,128)(2,1)}, u32[]{:S(2)}) copy-start(bf16[512,1024]{1,0:T(8,128)(2,1)} %get-tuple-element.307) | copy-start | bytes 3145732 | tf_op jit(solution)/shard_map/while
  96.6 12.3 %copy-start.1 = (bf16[512,1024]{1,0:T(8,128)(2,1)S(1)}, bf16[512,1024]{1,0:T(8,128)(2,1)}, u32[]{:S(2)}) copy-start(bf16[512,1024]{1,0:T(8,128)(2,1)} %get-tuple-element.307) | copy-start | bytes 3145732 | tf_op jit(solution)/shard_map/while
  115.8 12.3 %copy-start.1 = (bf16[512,1024]{1,0:T(8,128)(2,1)S(1)}, bf16[512,1024]{1,0:T(8,128)(2,1)}, u32[]{:S(2)}) copy-start(bf16[512,1024]{1,0:T(8,128)(2,1)} %get-tuple-element.307) | copy-start | bytes 3145732 | tf_op jit(solution)/shard_map/while
  134.9 12.3 %copy-start.1 = (bf16[512,1024]{1,0:T(8,128)(2,1)S(1)}, bf16[512,1024]{1,0:T(8,128)(2,1)}, u32[]{:S(2)}) copy-start(bf16[512,1024]{1,0:T(8,128)(2,1)} %get-tuple-element.307) | copy-start | bytes 3145732 | tf_op jit(solution)/shard_map/while
  154.1 12.3 %copy-start.1 = (bf16[512,1024]{1,0:T(8,128)(2,1)S(1)}, bf16[512,1024]{1,0:T(8,128)(2,1)}, u32[]{:S(2)}) copy-start(bf16[512,1024]{1,0:T(8,128)(2,1)} %get-tuple-element.307) | copy-start | bytes 3145732 | tf_op jit(solution)/shard_map/while
  173.3 1.4 copy-start
  174.6 82.2 %reduce-scatter.10.cloned.1.call-start = ((), (), s32[]{:S(2)}) async-start(), calls=%async_computation.6 | async-start | bytes 327680
  175.6 105.1 %reduce-scatter.8.cloned.1.call-start = ((), (), s32[]{:S(2)}) async-start(), calls=%async_computation.5 | async-start | bytes 655360 | tf_op jit(solution)/shard_map/reduce_scatter | solution.py:68
Sparse Core Ops, SparseCore 0:
  8.9 29.8 all-gather.1
  174.8 62.0 reduce-scatter.5
  239.2 17.5 reduce-scatter.9
  259.1 21.4 reduce-scatter.7
where the time goes:
time: 293 us; the launch traced here: 289 us
  waiting for transfers between devices  128 us (44%)
  matrix products  69 us (24%)
  loops' own time  53.9 us (18%)
  local copies, waits for them, and re-layouts  14.1 us (5%)
  between operations  13.8 us (5%)
  blocking collectives  7.32 us (2%)
    reduce_scatter x1, waiting for transfers between devices, per_device(): lax.psum_scatter(summed_rows, 'db', scatter_dimension=0, tiled=True)  61.2 us
    another operation x1, loops' own time, per_device(): summed_rows, total_rows = lax.fori_loop(0, turns, visit, start)  53.9 us
    dot_general x28, matrix products, visit(): lax.dot_general(query_tile, db_tile, (((1,), (1,)), ((), ())), preferred_...  35.2 us
    dot_general x28, matrix products, visit(): jnp.dot(weights.astype(jnp.bfloat16), db_tile, preferred_element_type=jnp...  33.8 us
    all_gather x1, waiting for transfers between devices, per_device(): panels = lax.all_gather(queries, 'db', axis=0, tiled=True)  30.9 us
    unnamed x5, waiting for transfers between devices  20.7 us
    reduce_scatter x1, waiting for transfers between devices, per_device(): lax.psum_scatter(row_sums, 'loop', scatter_dimension=1, tiled=True)  15.6 us
    dynamic_slice x7, local copies, waits for them, and re-layouts, visit(): db_start = slot_db[slot_no] * block_rows  10.7 us
  transfers between devices with their start and end apart: 4, of which 4 were waited for; matrix products, arithmetic and copies ran while one was open for 1% of the time, Pallas kernels for 0%

commit v1 on v0

v1 whole, which is shorter than its diff:
```python
import functools
import math

import jax
import jax.numpy as jnp
from jax import lax
from jax.experimental import pallas as pl
from jax.experimental.pallas import tpu as pltpu
from jax.sharding import PartitionSpec as P

BLK = 128
EXTRA = 16
score_gain = 2.0
WIRE = jnp.float16


def block_kernel(scale, meta, own_code, other_code, q_ref, db_ref, other_ref, send_ref, keep_ref,
                 acc, wacc, rows, listing, sems):
    block, side = meta[0], meta[1]
    slots = own_code.shape[1]

    def gather(code_ref, base):
        def step(j, n):
            code = code_ref[0, j]
            listing[n] = base + code % 16
            return n + (code // 16 == block).astype(jnp.int32)
        return step

    n_own = lax.fori_loop(0, slots, gather(own_code, 0), 0)
    n_all = lax.fori_loop(0, slots, gather(other_code, 16), n_own)
    listing[n_all] = listing[jnp.maximum(n_all - 1, 0)]
    steps = (n_all + 1) // 2

    def copy(i, ref):
        start = pl.multiple_of((listing[i] % 16) * BLK, BLK)
        to = pl.multiple_of(i * BLK, BLK)
        return pltpu.make_async_copy(ref.at[pl.ds(start, BLK)], rows.at[pl.ds(to, BLK)], sems.at[i])

    def issue(i, carry):
        @pl.when(listing[i] < 16)
        def _():
            copy(i, db_ref).start()

        @pl.when(listing[i] >= 16)
        def _():
            copy(i, other_ref).start()
        return carry

    lax.fori_loop(0, 2 * steps, issue, 0)
    acc[...] = jnp.zeros_like(acc)
    wacc[...] = jnp.zeros_like(wacc)

    def visit(i, carry):
        copy(2 * i, db_ref).wait()
        copy(2 * i + 1, db_ref).wait()
        tile = rows[pl.ds(pl.multiple_of(i * 2 * BLK, 2 * BLK), 2 * BLK), :]
        s = lax.dot_general(q_ref[...], tile, (((1,), (1,)), ((), ())), preferred_element_type=jnp.float32)
        w = 0.5 * jnp.tanh(s * (0.5 * scale)) + 0.5
        col = lax.broadcasted_iota(jnp.int32, w.shape, 1)
        w = jnp.where(col < (n_all - 2 * i) * BLK, w, 0.0)
        wacc[...] += w[:, :BLK] + w[:, BLK:]
        acc[...] += jnp.dot(w.astype(jnp.bfloat16), tile, preferred_element_type=jnp.float32)
        return carry

    lax.fori_loop(0, steps, visit, 0)
    width = send_ref.shape[1]
    away = pl.multiple_of((1 - side) * width, width)
    here = pl.multiple_of(side * width, width)
    send_ref[pl.ds(0, BLK), :] = acc[:, pl.ds(away, width)]
    keep_ref[pl.ds(0, BLK), :] = acc[:, pl.ds(here, width)]
    totals = jnp.sum(jnp.transpose(wacc[...]), axis=0, keepdims=True)
    totals = jnp.broadcast_to(totals, (EXTRA, BLK))
    totals = jnp.concatenate([totals] * (width // BLK), axis=1)
    send_ref[pl.ds(BLK, EXTRA), :] = totals
    keep_ref[pl.ds(BLK, EXTRA), :] = totals


def block_sums(meta, own_code, other_code, q, db, other, scale):
    width = q.shape[1]
    half = width // 2
    smem = pl.BlockSpec(memory_space=pltpu.SMEM)
    vmem = pl.BlockSpec(memory_space=pltpu.VMEM)
    hbm = pl.BlockSpec(memory_space=pl.ANY)
    most = 2 * own_code.shape[1] // 2 + 2
    return pl.pallas_call(
        functools.partial(block_kernel, scale),
        out_shape=(
            jax.ShapeDtypeStruct((BLK + EXTRA, half), jnp.float32),
            jax.ShapeDtypeStruct((BLK + EXTRA, half), jnp.float32),
        ),
        in_specs=[smem, smem, smem, vmem, hbm, hbm],
        out_specs=(vmem, vmem),
        scratch_shapes=[
            pltpu.VMEM((BLK, width), jnp.float32),
            pltpu.VMEM((BLK, BLK), jnp.float32),
            pltpu.VMEM((most * BLK, width), jnp.bfloat16),
            pltpu.SMEM((most + 2,), jnp.int32),
            pltpu.SemaphoreType.DMA((most,)),
        ],
        compiler_params=pltpu.CompilerParams(vmem_limit_bytes=32 * 1024 * 1024),
        cost_estimate=pl.CostEstimate(flops=2 * 2 * BLK * 2048 * width, bytes_accessed=4 * 1024 * 1024, transcendentals=BLK * 2048),
    )(meta, own_code, other_code, q, db, other)


def final_kernel(keep_ref, got_ref, q_ref, out_ref):
    s = keep_ref[...] + got_ref[...]
    totals = jnp.broadcast_to(s[BLK:BLK + 1, :BLK], (BLK, BLK))
    column = jnp.transpose(totals)
    factor = lax.rsqrt(1.0 + column)
    factor = jnp.concatenate([factor] * (out_ref.shape[1] // BLK), axis=1)
    out_ref[...] = q_ref[...].astype(jnp.float32) + s[:BLK] * factor


def paired(queries, database, pair_query, pair_db, pair_count):
    width = queries.shape[1]
    z = lax.axis_index("db")
    place = lax.axis_index("loop")
    side, core = place // 2, place % 2
    scale = score_gain / math.sqrt(width)
    core_swap = [(i, i ^ 1) for i in range(4)]
    side_swap = [(i, i ^ 2) for i in range(4)]
    near = [(4 * i + j, 4 * (i ^ (j & 1)) + j) for i in range(4) for j in range(4)]
    far = [(4 * i + j, 4 * (i ^ (2 + (j & 1))) + j) for i in range(4) for j in range(4)]
    both = ("db", "loop")

    slot = lax.broadcasted_iota(jnp.int32, pair_query.shape, 1)
    code = jnp.where(slot < pair_count[0], pair_query * 16 + pair_db, -16)
    other = lax.ppermute(database, "loop", core_swap)
    other_code = lax.ppermute(code, "loop", core_swap)
    first = lax.ppermute(queries, both, near)
    second = lax.ppermute(queries, both, far)
    meta1 = jnp.stack([z ^ core, side]).astype(jnp.int32)
    meta2 = jnp.stack([z ^ core ^ 2, side]).astype(jnp.int32)
    send1, keep1 = block_sums(meta1, code, other_code, first, database, other, scale)
    got1 = lax.ppermute(send1.astype(WIRE), "loop", side_swap)
    send2, keep2 = block_sums(meta2, code, other_code, second, database, other, scale)
    got2 = lax.ppermute(send2.astype(WIRE), "loop", side_swap)
    sum1 = (keep1 + got1.astype(jnp.float32)).astype(WIRE)
    in1 = lax.ppermute(sum1, both, near)
    sum2 = (keep2 + got2.astype(jnp.float32)).astype(WIRE)
    in2 = lax.ppermute(sum2, both, far)
    total = in1.astype(jnp.float32) + in2.astype(jnp.float32)
    quarter = width // 4
    given = (lax.dynamic_slice_in_dim(total, (1 - core) * quarter, quarter, 1) * 0.25).astype(WIRE)
    kept = lax.dynamic_slice_in_dim(total, core * quarter, quarter, 1)
    got = lax.ppermute(given, "loop", core_swap).astype(jnp.float32) * 4.0
    own = lax.dynamic_slice_in_dim(queries, place * quarter, quarter, 1)
    return pl.pallas_call(
        final_kernel,
        out_shape=jax.ShapeDtypeStruct((BLK, quarter), jnp.float32),
        in_specs=[pl.BlockSpec(memory_space=pltpu.VMEM)] * 3,
        out_specs=pl.BlockSpec(memory_space=pltpu.VMEM),
    )(kept, got, own)


def per_device(queries, database, pair_query, pair_db, pair_count):
    panels = lax.all_gather(queries, "db", axis=0, tiled=True)
    query_rows, feature_count = panels.shape
    score_scale = score_gain / math.sqrt(feature_count)
    slot_query, slot_db, live_count = pair_query[0], pair_db[0], pair_count[0]

    def visit(slot_no, state_pair):
        summed, totals = state_pair
        query_start = slot_query[slot_no] * BLK
        query_tile = lax.dynamic_slice_in_dim(panels, query_start, BLK, 0)
        db_tile = lax.dynamic_slice_in_dim(database, slot_db[slot_no] * BLK, BLK, 0)
        scores = lax.dot_general(
            query_tile, db_tile, (((1,), (1,)), ((), ())), preferred_element_type=jnp.float32
        ) * score_scale
        weights = jax.nn.sigmoid(scores)
        contrib = jnp.dot(weights.astype(jnp.bfloat16), db_tile, preferred_element_type=jnp.float32)
        old_rows = lax.dynamic_slice_in_dim(summed, query_start, BLK, 0)
        summed = lax.dynamic_update_slice_in_dim(summed, old_rows + contrib, query_start, 0)
        old_totals = lax.dynamic_slice_in_dim(totals, query_start, BLK, 0)
        totals = lax.dynamic_update_slice_in_dim(
            totals, old_totals + jnp.sum(weights, axis=1, keepdims=True), query_start, 0
        )
        return (summed, totals)

    start = (
        jnp.zeros((query_rows, feature_count), jnp.float32),
        jnp.zeros((query_rows, 1), jnp.float32),
    )
    summed_rows, total_rows = lax.fori_loop(0, live_count, visit, start)
    column_width = feature_count // lax.axis_size("loop")
    own_profiles = lax.dynamic_slice_in_dim(
        queries, lax.axis_index("loop") * column_width, column_width, 1
    ).astype(jnp.float32)
    row_sums = lax.psum_scatter(summed_rows, "db", scatter_dimension=0, tiled=True)
    row_weights = lax.psum_scatter(total_rows, "db", scatter_dimension=0, tiled=True)
    partial_out = lax.psum_scatter(row_sums, "loop", scatter_dimension=1, tiled=True)
    weight_out = lax.psum(row_weights, "loop")
    return own_profiles + partial_out * lax.rsqrt(1.0 + weight_out)


def solution(mesh):
    fits = mesh.shape["db"] == 4 and mesh.shape["loop"] == 4
    return jax.shard_map(
        paired if fits else per_device,
        mesh=mesh,
        in_specs=(
            P(("parts", "db"), None),
            P(("parts", "db", "loop"), None),
            P(("parts", "db", "loop"), None),
            P(("parts", "db", "loop"), None),
            P(("parts", "db", "loop")),
        ),
        out_specs=P(("parts", "db"), "loop"),
        check_vma=False,
    )
```

time: 293 us -> 47.3 us (0.16); the launches traced: 289 us -> 46.8 us
  waiting for transfers between devices: 128 us -> 9.44 us
  matrix products: 69 us -> 0 us
  loops' own time: 53.9 us -> 0 us
  starting transfers between devices: 0.12 us -> 17.6 us
  between operations: 13.8 us -> 0.72 us
  Pallas kernels: 0 us -> 13 us
  local copies, waits for them, and re-layouts: 14.1 us -> 3.66 us
  blocking collectives: 7.32 us -> 0 us
    reduce_scatter x2 -> x0, waiting for transfers between devices: 76.9 us -> none  [the longest x1 61.2 us: per_device(): lax.psum_scatter(summed_rows, 'db', scatter_dimension=0, tiled=True)]
    dot_general x56 -> x0, matrix products: 69 us -> none  [the longest x28 35.2 us: visit(): lax.dot_general(query_tile, db_tile, (((1,), (1,)), ((), ())), preferred_...]
    another operation x1 -> x0, loops' own time: 53.9 us -> none  [per_device(): summed_rows, total_rows = lax.fori_loop(0, turns, visit, start)]
    all_gather x1 -> x0, waiting for transfers between devices: 30.9 us -> none  [per_device(): panels = lax.all_gather(queries, 'db', axis=0, tiled=True)]
    unnamed x5 -> x0, waiting for transfers between devices: 20.7 us -> none
    ppermute x0 -> x9, starting transfers between devices: none -> 17.6 us  [the longest x1 4.64 us: paired(): first = lax.ppermute(queries, both, near)]
    pallas_call x0 -> x3, Pallas kernels: none -> 13 us  [the longest x2 11.3 us: block_sums(): pl.pallas_call(functools.partial(block_kernel, scale), out_shape=(jax.Sha...]
    ppermute x0 -> x9, waiting for transfers between devices: none -> 9.44 us  [the longest x1 5.64 us: paired(): in2 = lax.ppermute(sum2, both, far)]
  transfers between devices with their start and end apart: 4 -> 9, of which waited for: 4 -> 4; matrix products, arithmetic and copies ran while one was open for 1% -> 5% of each run, Pallas kernels for 0% -> 24%
where the time goes in v1:
time: 47.3 us; the launch traced here: 46.8 us
  starting transfers between devices  17.6 us (37%)
  Pallas kernels  13 us (27%)
  waiting for transfers between devices  9.44 us (20%)
  local copies, waits for them, and re-layouts  3.66 us (8%)
  other arithmetic  2.37 us (5%)
  between operations  0.72 us (2%)
    pallas_call x2, Pallas kernels, block_sums(): pl.pallas_call(functools.partial(block_kernel, scale), out_shape=(jax.Sha...  11.3 us
    ppermute x1, waiting for transfers between devices, paired(): in2 = lax.ppermute(sum2, both, far)  5.64 us
    ppermute x1, starting transfers between devices, paired(): first = lax.ppermute(queries, both, near)  4.64 us
    ppermute x1, starting transfers between devices, paired(): in2 = lax.ppermute(sum2, both, far)  4.25 us
    ppermute x1, starting transfers between devices, paired(): got2 = lax.ppermute(send2.astype(WIRE), 'loop', side_swap)  3.82 us
    ppermute x1, starting transfers between devices, paired(): second = lax.ppermute(queries, both, far)  2.26 us
    unnamed x4, local copies, waits for them, and re-layouts  2.19 us
    ppermute x1, starting transfers between devices, paired(): in1 = lax.ppermute(sum1, both, near)  2.17 us
  transfers between devices with their start and end apart: 9, of which 4 were waited for; matrix products, arithmetic and copies ran while one was open for 5% of the time, Pallas kernels for 24%

profile of v1, /device:TPU:1, one launch (start us, length us, event | category | flops | bytes accessed | tf_op | source)
XLA Modules:
  0.0 46.8 jit_solution(8059654270292604274)
XLA Ops:
  0.0 0.1 collective-permute-start.2
  0.1 4.6 %collective-permute-start.1 = (bf16[128,1024]{1,0:T(8,128)(2,1)}, bf16[128,1024]{1,0:T(8,128)(2,1)S(1)}, u32[]{:S(2)}, u32[]{:S(2)}) collective-permute-start(bf16[128,1024]{1,0:T(8,128)(2,1)} %param.5), channel_id=1, source_target_pairs={{0,0},{1,5},{2,2},{3,7},{4,4},{5,1},{6,6},{7,3},{8,8},{9,13},{10,1... | collective-permute-start | bytes 786440 | tf_op jit(solution)/shard_map/ppermute | solution.py:130
  4.7 2.3 %collective-permute-start.5 = (bf16[128,1024]{1,0:T(8,128)(2,1)}, bf16[128,1024]{1,0:T(8,128)(2,1)S(1)}, u32[]{:S(2)}, u32[]{:S(2)}) collective-permute-start(bf16[128,1024]{1,0:T(8,128)(2,1)} %param.5), channel_id=1, source_target_pairs={{0,8},{1,13},{2,10},{3,15},{4,12},{5,9},{6,14},{7,11},{8,0},{9,5},... | collective-permute-start | bytes 786440 | tf_op jit(solution)/shard_map/ppermute | solution.py:131
  7.6 0.7 %compare_select_fusion.own_code = s32[1,32]{1,0:T(1,128)S(1)} fusion(s32[1,32]{1,0:T(1,128)} %param.8, s32[1,32]{1,0:T(1,128)} %param.7, s32[]{:T(128)} %bitcast.4), kind=kLoop, calls=%fused_computation.5 | loop fusion | flops 128 | bytes 388 | tf_op jit(solution)/shard_map/jit(_where)/select_n | solution.py:127
  8.3 0.0 collective-permute-start
  8.3 0.1 pad_add_fusion.meta
  8.4 1.0 %collective-permute-done.other_code = s32[1,32]{1,0:T(1,128)S(1)} collective-permute-done((s32[1,32]{1,0:T(1,128)S(1)}, s32[1,32]{1,0:T(1,128)S(1)}, u32[]{:S(2)}, u32[]{:S(2)}) %collective-permute-start) | collective-permute-done | bytes 160 | tf_op jit(solution)/shard_map/ppermute | solution.py:129
  9.4 1.5 %collective-permute-done.1.q_ref = bf16[128,1024]{1,0:T(8,128)(2,1)S(1)} collective-permute-done((bf16[128,1024]{1,0:T(8,128)(2,1)}, bf16[128,1024]{1,0:T(8,128)(2,1)S(1)}, u32[]{:S(2)}, u32[]{:S(2)}) %collective-permute-start.1) | collective-permute-done | bytes 262176 | tf_op jit(solution)/shard_map/ppermute | solution.py:130
  11.0 0.0 collective-permute-done.2.other_ref
  11.0 0.0 copy-start
  11.0 2.2 %copy-done = bf16[2048,1024]{1,0:T(8,128)(2,1)S(1)} copy-done((bf16[2048,1024]{1,0:T(8,128)(2,1)S(1)}, bf16[2048,1024]{1,0:T(8,128)(2,1)}, u32[]{:S(2)}) %copy-start) | copy-done | bytes 4194328
  13.2 0.0 copy-start.1
  13.2 5.9 %shard_map.55 = (f32[144,512]{1,0:T(8,128)S(1)}, f32[144,512]{1,0:T(8,128)S(1)}) custom-call(s32[2]{0:T(128)S(1)} %pad_add_fusion.meta, s32[1,32]{1,0:T(1,128)S(1)} %compare_select_fusion.own_code, s32[1,32]{1,0:T(1,128)S(1)} %collective-permute-done.other_code, bf16[128,1024]{1,0:T(8,128)(2,1)S(1)} %collective-permute-done.1.q_ref, ...), custom_call_target="tpu_custom_call" | custom-call | flops 1073741824 | bytes 4194304 | tf_op jit(solution)/shard_map/pallas_call | solution.py:85
  19.1 0.4 collective-permute-start.3
  19.5 0.1 pad_add_fusion.1.meta
  19.6 0.0 collective-permute-done.5.q_ref
  19.6 0.0 copy-done.1
  19.6 5.4 %shard_map.56 = (f32[144,512]{1,0:T(8,128)S(1)}, f32[144,512]{1,0:T(8,128)S(1)}) custom-call(s32[2]{0:T(128)S(1)} %pad_add_fusion.1.meta, s32[1,32]{1,0:T(1,128)S(1)} %compare_select_fusion.own_code, s32[1,32]{1,0:T(1,128)S(1)} %collective-permute-done.other_code, bf16[128,1024]{1,0:T(8,128)(2,1)S(1)} %collective-permute-done.5.q_ref, ...), custom_call_target="tpu_custom_call" | custom-call | flops 1073741824 | bytes 4194304 | tf_op jit(solution)/shard_map/pallas_call | solution.py:85
  25.0 3.8 %collective-permute-start.6 = (f16[144,512]{1,0:T(8,128)(2,1)S(1)}, f16[144,512]{1,0:T(8,128)(2,1)S(1)}, u32[]{:S(2)}, u32[]{:S(2)}) collective-permute-start(f16[144,512]{1,0:T(8,128)(2,1)S(1)} %convert_element_type.34), channel_id=1, source_target_pairs={{0,2},{1,3},{2,0},{3,1},{4,6},{5,7},{6,4},{7,5},{8,10},{9,11},{10,... | collective-permute-start | bytes 442376 | tf_op jit(solution)/shard_map/ppermute | solution.py:137
  28.8 0.0 collective-permute-done.3
  28.8 0.1 add_convert_fusion.1
  28.9 2.2 %collective-permute-start.4 = (f16[144,512]{1,0:T(8,128)(2,1)S(1)}, f16[144,512]{1,0:T(8,128)(2,1)S(1)}, u32[]{:S(2)}, u32[]{:S(2)}) collective-permute-start(f16[144,512]{1,0:T(8,128)(2,1)S(1)} %add_convert_fusion.1), channel_id=1, source_target_pairs={{0,0},{1,5},{2,2},{3,7},{4,4},{5,1},{6,6},{7,3},{8,8},{9,13},{10,1... | collective-permute-start | bytes 442376 | tf_op jit(solution)/shard_map/ppermute | solution.py:139
  31.0 1.2 %collective-permute-done.6 = f16[144,512]{1,0:T(8,128)(2,1)S(1)} collective-permute-done((f16[144,512]{1,0:T(8,128)(2,1)S(1)}, f16[144,512]{1,0:T(8,128)(2,1)S(1)}, u32[]{:S(2)}, u32[]{:S(2)}) %collective-permute-start.6) | collective-permute-done | bytes 147488 | tf_op jit(solution)/shard_map/ppermute | solution.py:137
  32.3 4.2 %collective-permute-start.7 = (f16[144,512]{1,0:T(8,128)(2,1)S(1)}, f16[144,512]{1,0:T(8,128)(2,1)S(1)}, u32[]{:S(2)}, u32[]{:S(2)}) collective-permute-start(f16[144,512]{1,0:T(8,128)(2,1)S(1)} %add_convert_fusion), channel_id=1, source_target_pairs={{0,8},{1,13},{2,10},{3,15},{4,12},{5,9},{6,14},{7,11},{8,0},{9,5},... | collective-permute-start | bytes 442376 | tf_op jit(solution)/shard_map/ppermute | solution.py:141
  36.5 0.0 collective-permute-done.4
  36.5 5.6 %collective-permute-done.7 = f16[144,512]{1,0:T(8,128)(2,1)S(1)} collective-permute-done((f16[144,512]{1,0:T(8,128)(2,1)S(1)}, f16[144,512]{1,0:T(8,128)(2,1)S(1)}, u32[]{:S(2)}, u32[]{:S(2)}) %collective-permute-start.7) | collective-permute-done | bytes 147488 | tf_op jit(solution)/shard_map/ppermute | solution.py:141
  42.2 0.7 %multiply_convert_fusion = (f16[144,256]{1,0:T(8,128)(2,1)S(1)}, f32[144,256]{1,0:T(8,128)}) fusion(f32[144,512]{1,0:T(8,128)S(1)} %convert_add_fusion, s32[]{:T(128)S(6)} %select_n.28, s32[]{:T(128)S(6)} %select_n.27), kind=kLoop, calls=%fused_computation.4 | loop fusion | flops 73728 | bytes 516104 | tf_op jit(solution)/shard_map/convert_element_type | solution.py:144
  42.9 0.0 collective-permute-start.8
  42.9 1.5 %constant_dynamic-slice_fusion.q_ref = bf16[128,256]{1,0:T(8,128)(2,1)} fusion(bf16[128,1024]{1,0:T(8,128)(2,1)} %param.5, s32[]{:T(128)S(6)} %select_n.29), kind=kLoop, calls=%fused_computation.6 | loop fusion | bytes 131076 | tf_op jit(solution)/shard_map/dynamic_slice | solution.py:147
  44.4 0.0 collective-permute-done.8
  44.4 0.7 %convert_multiply_fusion.got_ref = f32[144,256]{1,0:T(8,128)} fusion(f16[144,256]{1,0:T(8,128)(2,1)S(1)} %collective-permute-done.8), kind=kLoop, calls=%fused_computation.3 | loop fusion | flops 73728 | bytes 221184 | tf_op jit(solution)/shard_map/mul | solution.py:146
  45.0 1.7 %shard_map.57 = f32[128,256]{1,0:T(8,128)} custom-call(f32[144,256]{1,0:T(8,128)} %get-tuple-element.14.keep_ref, f32[144,256]{1,0:T(8,128)} %convert_multiply_fusion.got_ref, bf16[128,256]{1,0:T(8,128)(2,1)} %constant_dynamic-slice_fusion.q_ref), custom_call_target="tpu_custom_call" | custom-call | tf_op jit(solution)/shard_map/pallas_call | solution.py:148
  (4 shorter events, 0.1 us)
Async XLA Ops:
  0.0 11.0 %collective-permute-start.2 = (bf16[2048,1024]{1,0:T(8,128)(2,1)}, bf16[2048,1024]{1,0:T(8,128)(2,1)}, u32[]{:S(2)}, u32[]{:S(2)}) collective-permute-start(bf16[2048,1024]{1,0:T(8,128)(2,1)} %db_ref.3), channel_id=1, source_target_pairs={{0,1},{1,0},{2,3},{3,2},{4,5},{5,4},{6,7},{7,6},{8,9},{9,8},{10,11... | collective-permute-start | bytes 12582920 | tf_op jit(solution)/shard_map/ppermute | solution.py:128
  0.1 10.9 %collective-permute-start.1 = (bf16[128,1024]{1,0:T(8,128)(2,1)}, bf16[128,1024]{1,0:T(8,128)(2,1)S(1)}, u32[]{:S(2)}, u32[]{:S(2)}) collective-permute-start(bf16[128,1024]{1,0:T(8,128)(2,1)} %param.5), channel_id=1, source_target_pairs={{0,0},{1,5},{2,2},{3,7},{4,4},{5,1},{6,6},{7,3},{8,8},{9,13},{10,1... | collective-permute-start | bytes 786440 | tf_op jit(solution)/shard_map/ppermute | solution.py:130
  4.7 14.8 %collective-permute-start.5 = (bf16[128,1024]{1,0:T(8,128)(2,1)}, bf16[128,1024]{1,0:T(8,128)(2,1)S(1)}, u32[]{:S(2)}, u32[]{:S(2)}) collective-permute-start(bf16[128,1024]{1,0:T(8,128)(2,1)} %param.5), channel_id=1, source_target_pairs={{0,8},{1,13},{2,10},{3,15},{4,12},{5,9},{6,14},{7,11},{8,0},{9,5},... | collective-permute-start | bytes 786440 | tf_op jit(solution)/shard_map/ppermute | solution.py:131
  8.3 1.1 %collective-permute-start = (s32[1,32]{1,0:T(1,128)S(1)}, s32[1,32]{1,0:T(1,128)S(1)}, u32[]{:S(2)}, u32[]{:S(2)}) collective-permute-start(s32[1,32]{1,0:T(1,128)S(1)} %compare_select_fusion.own_code), channel_id=1, source_target_pairs={{0,1},{1,0},{2,3},{3,2},{4,5},{5,4},{6,7},{7,6},{8,9},{9,8},{10,11... | collective-permute-start | bytes 392 | tf_op jit(solution)/shard_map/ppermute | solution.py:129
  11.0 2.2 %copy-start = (bf16[2048,1024]{1,0:T(8,128)(2,1)S(1)}, bf16[2048,1024]{1,0:T(8,128)(2,1)}, u32[]{:S(2)}) copy-start(bf16[2048,1024]{1,0:T(8,128)(2,1)} %db_ref.3) | copy-start | bytes 12582916
  13.2 6.4 %copy-start.1 = (bf16[2048,1024]{1,0:T(8,128)(2,1)S(1)}, bf16[2048,1024]{1,0:T(8,128)(2,1)}, u32[]{:S(2)}) copy-start(bf16[2048,1024]{1,0:T(8,128)(2,1)} %db_ref.3) | copy-start | bytes 12582916
  19.1 9.7 %collective-permute-start.3 = (f16[144,512]{1,0:T(8,128)(2,1)S(1)}, f16[144,512]{1,0:T(8,128)(2,1)S(1)}, u32[]{:S(2)}, u32[]{:S(2)}) collective-permute-start(f16[144,512]{1,0:T(8,128)(2,1)S(1)} %convert_element_type.30), channel_id=1, source_target_pairs={{0,2},{1,3},{2,0},{3,1},{4,6},{5,7},{6,4},{7,5},{8,10},{9,11},{10,... | collective-permute-start | bytes 442376 | tf_op jit(solution)/shard_map/ppermute | solution.py:135
  25.0 7.3 %collective-permute-start.6 = (f16[144,512]{1,0:T(8,128)(2,1)S(1)}, f16[144,512]{1,0:T(8,128)(2,1)S(1)}, u32[]{:S(2)}, u32[]{:S(2)}) collective-permute-start(f16[144,512]{1,0:T(8,128)(2,1)S(1)} %convert_element_type.34), channel_id=1, source_target_pairs={{0,2},{1,3},{2,0},{3,1},{4,6},{5,7},{6,4},{7,5},{8,10},{9,11},{10,... | collective-permute-start | bytes 442376 | tf_op jit(solution)/shard_map/ppermute | solution.py:137
  28.9 7.7 %collective-permute-start.4 = (f16[144,512]{1,0:T(8,128)(2,1)S(1)}, f16[144,512]{1,0:T(8,128)(2,1)S(1)}, u32[]{:S(2)}, u32[]{:S(2)}) collective-permute-start(f16[144,512]{1,0:T(8,128)(2,1)S(1)} %add_convert_fusion.1), channel_id=1, source_target_pairs={{0,0},{1,5},{2,2},{3,7},{4,4},{5,1},{6,6},{7,3},{8,8},{9,13},{10,1... | collective-permute-start | bytes 442376 | tf_op jit(solution)/shard_map/ppermute | solution.py:139
  32.3 9.9 %collective-permute-start.7 = (f16[144,512]{1,0:T(8,128)(2,1)S(1)}, f16[144,512]{1,0:T(8,128)(2,1)S(1)}, u32[]{:S(2)}, u32[]{:S(2)}) collective-permute-start(f16[144,512]{1,0:T(8,128)(2,1)S(1)} %add_convert_fusion), channel_id=1, source_target_pairs={{0,8},{1,13},{2,10},{3,15},{4,12},{5,9},{6,14},{7,11},{8,0},{9,5},... | collective-permute-start | bytes 442376 | tf_op jit(solution)/shard_map/ppermute | solution.py:141
  42.9 1.5 %collective-permute-start.8 = (f16[144,256]{1,0:T(8,128)(2,1)S(1)}, f16[144,256]{1,0:T(8,128)(2,1)S(1)}, u32[]{:S(2)}, u32[]{:S(2)}) collective-permute-start(f16[144,256]{1,0:T(8,128)(2,1)S(1)} %get-tuple-element.13), channel_id=1, source_target_pairs={{0,1},{1,0},{2,3},{3,2},{4,5},{5,4},{6,7},{7,6},{8,9},{9,8},{10,11... | collective-permute-start | bytes 221192 | tf_op jit(solution)/shard_map/ppermute | solution.py:146

commit v2 on v0

v2 whole, which is shorter than its diff:
```python
import functools
import math

import jax
import jax.numpy as jnp
from jax import lax
from jax.experimental import pallas as pl
from jax.experimental.pallas import tpu as pltpu
from jax.sharding import PartitionSpec as P

BLK = 128
EXTRA = 8
score_gain = 2.0
WIRE = jnp.float16
SMEM = pl.BlockSpec(memory_space=pltpu.SMEM)
VMEM = pl.BlockSpec(memory_space=pltpu.VMEM)
HBM = pl.BlockSpec(memory_space=pltpu.MemorySpace.HBM)
CHUNKS = 4


def plan_kernel(blocks, meta, own_code, other_code, db_ref, other_ref, rows_ref, plan_ref, sems):
    part = db_ref.shape[0] // CHUNKS
    copies = []
    for shard, ref in enumerate((db_ref, other_ref)):
        for i in range(CHUNKS):
            copies.append(pltpu.make_async_copy(
                ref.at[pl.ds(i * part, part)],
                rows_ref.at[pl.ds((shard * CHUNKS + i) * part, part)],
                sems.at[shard * CHUNKS + i],
            ))
    for copy in copies:
        copy.start()
    slots = own_code.shape[1]
    last = plan_ref.shape[1] - 1
    for which in range(2):
        block = meta[which]
        n = jnp.int32(0)
        for code_ref, base in ((own_code, 0), (other_code, blocks)):
            def step(j, n, code_ref=code_ref, base=base):
                code = code_ref[0, j]
                plan_ref[which, n] = base + (code & 255)
                return n + ((code >> 8) == block).astype(jnp.int32)
            n = lax.fori_loop(0, slots, step, n)
        final = plan_ref[which, jnp.maximum(n - 1, 0)]
        final = jnp.where(n > 0, final, 0)
        for i in range(8):
            plan_ref[which, n + i] = final
        plan_ref[which, last] = n
    for copy in copies:
        copy.wait()


def make_plan(meta, own_code, other_code, db, other):
    slots = own_code.shape[1]
    return pl.pallas_call(
        functools.partial(plan_kernel, db.shape[0] // BLK),
        out_shape=(
            jax.ShapeDtypeStruct((2 * db.shape[0], db.shape[1]), db.dtype),
            jax.ShapeDtypeStruct((2, 2 * slots + 16), jnp.int32),
        ),
        in_specs=[SMEM, SMEM, SMEM, HBM, HBM],
        out_specs=(VMEM, SMEM),
        scratch_shapes=[pltpu.SemaphoreType.DMA((2 * CHUNKS,))],
        compiler_params=pltpu.CompilerParams(vmem_limit_bytes=24 * 1024 * 1024),
        name="plan",
    )(meta, own_code, other_code, db, other)


def block_kernel(scale, which, meta, plan, q_ref, rows_ref, send_ref, keep_ref, acc, wacc):
    side, core = meta[2], meta[3]
    n = plan[which, plan.shape[1] - 1]
    acc[...] = jnp.zeros_like(acc)
    wacc[...] = jnp.zeros_like(wacc)

    def visit(first, group):
        tiles = []
        for g in range(group):
            start = pl.multiple_of(plan[which, first + g] * BLK, BLK)
            tiles.append(rows_ref[pl.ds(start, BLK), :])
        tile = jnp.concatenate(tiles, 0)
        s = lax.dot_general(q_ref[...], tile, (((1,), (1,)), ((), ())), preferred_element_type=jnp.float32)
        w = 0.5 * jnp.tanh(s * (0.5 * scale)) + 0.5
        col = lax.broadcasted_iota(jnp.int32, w.shape, 1)
        w = jnp.where(col < (n - first) * BLK, w, 0.0)
        wsum = wacc[...]
        for g in range(group):
            wsum = wsum + w[:, g * BLK:(g + 1) * BLK]
        wacc[...] = wsum
        acc[...] += jnp.dot(w.astype(jnp.bfloat16), tile, preferred_element_type=jnp.float32)

    wide = (n + 3) // 8

    def step(i, carry):
        visit(8 * i, 8)
        return carry

    lax.fori_loop(0, wide, step, 0)

    @pl.when(8 * wide < n)
    def _():
        visit(8 * wide, 4)

    half = send_ref.shape[1]
    piece = half // 2
    totals = jnp.sum(jnp.transpose(wacc[...]), axis=0, keepdims=True)
    totals = jnp.broadcast_to(totals, (EXTRA, BLK))
    totals = jnp.concatenate([totals] * (piece // BLK), axis=1)
    for ref, x in ((send_ref, 1 - side), (keep_ref, side)):
        for p, c in ((0, core), (1, 1 - core)):
            start = pl.multiple_of(x * half + c * piece, piece)
            ref[pl.ds(0, BLK), pl.ds(p * piece, piece)] = acc[:, pl.ds(start, piece)]
            ref[pl.ds(BLK, EXTRA), pl.ds(p * piece, piece)] = totals


def block_sums(which, meta, plan, q, rows, scale):
    width = q.shape[1]
    half = jax.ShapeDtypeStruct((BLK + EXTRA, width // 2), jnp.float32)
    return pl.pallas_call(
        functools.partial(block_kernel, scale, which),
        out_shape=(half, half),
        in_specs=[SMEM, SMEM, VMEM, VMEM],
        out_specs=(VMEM, VMEM),
        scratch_shapes=[
            pltpu.VMEM((BLK, width), jnp.float32),
            pltpu.VMEM((BLK, BLK), jnp.float32),
        ],
        compiler_params=pltpu.CompilerParams(vmem_limit_bytes=24 * 1024 * 1024),
        cost_estimate=pl.CostEstimate(
            flops=2 * 2 * BLK * 2048 * width, bytes_accessed=1024 * 1024, transcendentals=BLK * 2048),
        name=f"block{which}",
    )(meta, plan, q, rows)


def paired(queries, database, pair_query, pair_db, pair_count):
    width = queries.shape[1]
    z = lax.axis_index("db")
    place = lax.axis_index("loop")
    side, core = place // 2, place % 2
    scale = score_gain / math.sqrt(width)
    both = ("db", "loop")
    grid = [(i, j) for i in range(4) for j in range(4)]
    core_swap = [(j, j ^ 1) for j in range(4)]
    side_swap = [(j, j ^ 2) for j in range(4)]

    def hop(base, turn):
        return [(4 * i + j, 4 * (i ^ (base + (j & 1))) + (j ^ turn)) for i, j in grid]

    slot = lax.broadcasted_iota(jnp.int32, pair_query.shape, 1)
    code = jnp.where(slot < pair_count[0], pair_query * 256 + pair_db, -256)
    other = lax.ppermute(database, "loop", core_swap)
    second = lax.ppermute(queries, both, hop(2, 0))
    first = lax.ppermute(queries, both, hop(0, 0))
    other_code = lax.ppermute(code, "loop", core_swap)
    meta = jnp.stack([z ^ core, z ^ core ^ 2, side, core]).astype(jnp.int32)
    rows, plan = make_plan(meta, code, other_code, database, other)

    send1, keep1 = block_sums(0, meta, plan, first, rows, scale)
    send2, keep2 = block_sums(1, meta, plan, second, rows, scale)
    got1 = lax.ppermute(send1.astype(WIRE), "loop", side_swap)
    got2 = lax.ppermute(send2.astype(WIRE), "loop", side_swap)
    sum2 = (keep2 + got2.astype(jnp.float32)).astype(WIRE)
    sum1 = (keep1 + got1.astype(jnp.float32)).astype(WIRE)
    piece = width // 4
    parts = [
        lax.ppermute(sum2[:, :piece], both, hop(2, 0)),
        lax.ppermute(sum2[:, piece:], both, hop(2, 1)),
        lax.ppermute(sum1[:, :piece], both, hop(0, 0)),
        lax.ppermute(sum1[:, piece:], both, hop(0, 1)),
    ]
    parts = [p.astype(jnp.float32) for p in parts]
    total = (parts[2] + parts[3]) + (parts[0] + parts[1])
    own = lax.dynamic_slice_in_dim(queries, place * piece, piece, 1).astype(jnp.float32)
    return own + total[:BLK] * lax.rsqrt(1.0 + total[BLK, :BLK])[:, None]


def per_device(queries, database, pair_query, pair_db, pair_count):
    if lax.axis_size("db") == 4 and lax.axis_size("loop") == 4 and queries.shape[0] == BLK:
        return paired(queries, database, pair_query, pair_db, pair_count)
    panels = lax.all_gather(queries, "db", axis=0, tiled=True)
    query_rows, feature_count = panels.shape
    score_scale = score_gain / math.sqrt(feature_count)
    slot_query, slot_db, live_count = pair_query[0], pair_db[0], pair_count[0]

    def visit(slot_no, state_pair):
        summed, totals = state_pair
        query_start = slot_query[slot_no] * BLK
        query_tile = lax.dynamic_slice_in_dim(panels, query_start, BLK, 0)
        db_tile = lax.dynamic_slice_in_dim(database, slot_db[slot_no] * BLK, BLK, 0)
        scores = lax.dot_general(
            query_tile, db_tile, (((1,), (1,)), ((), ())), preferred_element_type=jnp.float32
        ) * score_scale
        weights = jax.nn.sigmoid(scores)
        contrib = jnp.dot(weights.astype(jnp.bfloat16), db_tile, preferred_element_type=jnp.float32)
        old_rows = lax.dynamic_slice_in_dim(summed, query_start, BLK, 0)
        summed = lax.dynamic_update_slice_in_dim(summed, old_rows + contrib, query_start, 0)
        old_totals = lax.dynamic_slice_in_dim(totals, query_start, BLK, 0)
        totals = lax.dynamic_update_slice_in_dim(
            totals, old_totals + jnp.sum(weights, axis=1, keepdims=True), query_start, 0
        )
        return (summed, totals)

    start = (
        jnp.zeros((query_rows, feature_count), jnp.float32),
        jnp.zeros((query_rows, 1), jnp.float32),
    )
    summed_rows, total_rows = lax.fori_loop(0, live_count, visit, start)
    column_width = feature_count // lax.axis_size("loop")
    own_profiles = lax.dynamic_slice_in_dim(
        queries, lax.axis_index("loop") * column_width, column_width, 1
    ).astype(jnp.float32)
    row_sums = lax.psum_scatter(summed_rows, "db", scatter_dimension=0, tiled=True)
    row_weights = lax.psum_scatter(total_rows, "db", scatter_dimension=0, tiled=True)
    partial_out = lax.psum_scatter(row_sums, "loop", scatter_dimension=1, tiled=True)
    weight_out = lax.psum(row_weights, "loop")
    return own_profiles + partial_out * lax.rsqrt(1.0 + weight_out)


def solution(mesh):
    return jax.shard_map(
        per_device,
        mesh=mesh,
        in_specs=(
            P(("parts", "db"), None),
            P(("parts", "db", "loop"), None),
            P(("parts", "db", "loop"), None),
            P(("parts", "db", "loop"), None),
            P(("parts", "db", "loop")),
        ),
        out_specs=P(("parts", "db"), "loop"),
        check_vma=False,
    )
```

time: 293 us -> 39.3 us (0.13); the launches traced: 289 us -> 38.8 us
  waiting for transfers between devices: 128 us -> 8.56 us
  matrix products: 69 us -> 0 us
  loops' own time: 53.9 us -> 0 us
  starting transfers between devices: 0.12 us -> 15 us
  between operations: 13.8 us -> 0.77 us
  local copies, waits for them, and re-layouts: 14.1 us -> 2.24 us
  Pallas kernels: 0 us -> 9.72 us
  blocking collectives: 7.32 us -> 0 us
    reduce_scatter x2 -> x0, waiting for transfers between devices: 76.9 us -> none  [the longest x1 61.2 us: per_device(): lax.psum_scatter(summed_rows, 'db', scatter_dimension=0, tiled=True)]
    dot_general x56 -> x0, matrix products: 69 us -> none  [the longest x28 35.2 us: visit(): lax.dot_general(query_tile, db_tile, (((1,), (1,)), ((), ())), preferred_...]
    another operation x1 -> x0, loops' own time: 53.9 us -> none  [per_device(): summed_rows, total_rows = lax.fori_loop(0, turns, visit, start)]
    all_gather x1 -> x0, waiting for transfers between devices: 30.9 us -> none  [per_device(): panels = lax.all_gather(queries, 'db', axis=0, tiled=True)]
    unnamed x5 -> x0, waiting for transfers between devices: 20.7 us -> none
    ppermute x0 -> x10, starting transfers between devices: none -> 15 us  [the longest x1 4.64 us: paired(): first = lax.ppermute(queries, both, hop(0, 0))]
    dynamic_slice x7 -> x0, local copies, waits for them, and re-layouts: 10.7 us -> none  [visit(): db_start = slot_db[slot_no] * block_rows]
    pallas_call x0 -> x3, Pallas kernels: none -> 9.72 us  [the longest x2 6.05 us: block_sums(): pl.pallas_call(functools.partial(block_kernel, scale, which), out_shape=(...]
  transfers between devices with their start and end apart: 4 -> 10, of which waited for: 4 -> 5; matrix products, arithmetic and copies ran while one was open for 1% -> 2% of each run, Pallas kernels for 0% -> 25%
where the time goes in v2:
time: 39.3 us; the launch traced here: 38.8 us
  starting transfers between devices  15 us (38%)
  Pallas kernels  9.72 us (25%)
  waiting for transfers between devices  8.56 us (22%)
  other arithmetic  2.53 us (6%)
  local copies, waits for them, and re-layouts  2.24 us (6%)
  between operations  0.77 us (2%)
    pallas_call x2, Pallas kernels, block_sums(): pl.pallas_call(functools.partial(block_kernel, scale, which), out_shape=(...  6.05 us
    ppermute x1, starting transfers between devices, paired(): first = lax.ppermute(queries, both, hop(0, 0))  4.64 us
    ppermute x1, waiting for transfers between devices, paired(): lax.ppermute(sum2[:, piece:], both, hop(2, 1))  4.49 us
    pallas_call x1, Pallas kernels, make_plan(): pl.pallas_call(functools.partial(plan_kernel, db.shape[0] // BLK), out_sh...  3.68 us
    ppermute x1, starting transfers between devices, paired(): lax.ppermute(sum1[:, :piece], both, hop(0, 0))  2.75 us
    ppermute x1, starting transfers between devices, paired(): second = lax.ppermute(queries, both, hop(2, 0))  2.26 us
    unnamed x2, local copies, waits for them, and re-layouts  2.19 us
    ppermute x1, starting transfers between devices, paired(): lax.ppermute(sum2[:, piece:], both, hop(2, 1))  2.13 us
  transfers between devices with their start and end apart: 10, of which 5 were waited for; matrix products, arithmetic and copies ran while one was open for 2% of the time, Pallas kernels for 25%

profile of v2, /device:TPU:1, one launch (start us, length us, event | category | flops | bytes accessed | tf_op | source)
XLA Modules:
  0.0 38.8 jit_solution(2037770602603664082)
XLA Ops:
  0.0 0.1 collective-permute-start.1
  0.1 4.6 %collective-permute-start.2 = (bf16[128,1024]{1,0:T(8,128)(2,1)}, bf16[128,1024]{1,0:T(8,128)(2,1)S(1)}, u32[]{:S(2)}, u32[]{:S(2)}) collective-permute-start(bf16[128,1024]{1,0:T(8,128)(2,1)} %param.5), channel_id=1, source_target_pairs={{0,0},{1,5},{2,2},{3,7},{4,4},{5,1},{6,6},{7,3},{8,8},{9,13},{10,1... | collective-permute-start | bytes 786440 | tf_op jit(solution)/shard_map/ppermute | solution.py:152
  4.7 2.3 %collective-permute-start.6 = (bf16[128,1024]{1,0:T(8,128)(2,1)}, bf16[128,1024]{1,0:T(8,128)(2,1)S(1)}, u32[]{:S(2)}, u32[]{:S(2)}) collective-permute-start(bf16[128,1024]{1,0:T(8,128)(2,1)} %param.5), channel_id=1, source_target_pairs={{0,8},{1,13},{2,10},{3,15},{4,12},{5,9},{6,14},{7,11},{8,0},{9,5},... | collective-permute-start | bytes 786440 | tf_op jit(solution)/shard_map/ppermute | solution.py:151
  7.6 0.7 %compare_select_fusion.own_code = s32[1,32]{1,0:T(1,128)S(1)} fusion(s32[1,32]{1,0:T(1,128)} %param.8, s32[1,32]{1,0:T(1,128)} %param.7, s32[]{:T(128)} %bitcast.7), kind=kLoop, calls=%fused_computation.5 | loop fusion | flops 128 | bytes 388 | tf_op jit(solution)/shard_map/jit(_where)/select_n | solution.py:149
  8.3 0.0 collective-permute-start
  8.3 0.1 pad_add_fusion.meta
  8.4 1.0 %collective-permute-done.other_code = s32[1,32]{1,0:T(1,128)S(1)} collective-permute-done((s32[1,32]{1,0:T(1,128)S(1)}, s32[1,32]{1,0:T(1,128)S(1)}, u32[]{:S(2)}, u32[]{:S(2)}) %collective-permute-start) | collective-permute-done | bytes 160 | tf_op jit(solution)/shard_map/ppermute | solution.py:153
  9.4 0.0 collective-permute-done.1.other_ref
  9.4 0.0 copy-start
  9.4 2.2 %copy-done = bf16[2048,1024]{1,0:T(8,128)(2,1)S(1)} copy-done((bf16[2048,1024]{1,0:T(8,128)(2,1)S(1)}, bf16[2048,1024]{1,0:T(8,128)(2,1)}, u32[]{:S(2)}) %copy-start) | copy-done | bytes 4194328
  11.6 3.7 %plan.1 = (bf16[4096,1024]{1,0:T(8,128)(2,1)S(1)}, s32[2,80]{1,0:T(2,128)S(1)}) custom-call(s32[4]{0:T(128)S(1)} %pad_add_fusion.meta, s32[1,32]{1,0:T(1,128)S(1)} %compare_select_fusion.own_code, s32[1,32]{1,0:T(1,128)S(1)} %collective-permute-done.other_code, bf16[2048,1024]{1,0:T(8,128)(2,1)S(1)} %copy-done, ...), custom_call_target="tpu_custom_call" | custom-call | tf_op jit(solution)/shard_map/plan/pallas_call | solution.py:55
  15.3 0.0 collective-permute-done.2.q_ref
  15.3 3.0 %block0.1 = (f32[136,512]{1,0:T(8,128)S(1)}, f32[136,512]{1,0:T(8,128)S(1)}) custom-call(s32[4]{0:T(128)S(1)} %pad_add_fusion.meta, s32[2,80]{1,0:T(2,128)S(1)} %get-tuple-element.11.plan, bf16[128,1024]{1,0:T(8,128)(2,1)S(1)} %collective-permute-done.2.q_ref, bf16[4096,1024]{1,0:T(8,128)(2,1)S(1)} %get-tuple-element.12.rows_ref), custom_call_target="tpu_custom_call" | custom-call | flops 1073741824 | bytes 1048576 | tf_op jit(solution)/shard_map/block0/pallas_call | solution.py:118
  18.4 1.3 %collective-permute-start.3 = (f16[136,512]{1,0:T(8,128)(2,1)S(1)}, f16[136,512]{1,0:T(8,128)(2,1)S(1)}, u32[]{:S(2)}, u32[]{:S(2)}) collective-permute-start(f16[136,512]{1,0:T(8,128)(2,1)S(1)} %convert_element_type.34), channel_id=1, source_target_pairs={{0,2},{1,3},{2,0},{3,1},{4,6},{5,7},{6,4},{7,5},{8,10},{9,11},{10,... | collective-permute-start | bytes 417800 | tf_op jit(solution)/shard_map/ppermute | solution.py:159
  19.7 0.0 collective-permute-done.6.q_ref
  19.7 3.0 %block1.1 = (f32[136,512]{1,0:T(8,128)S(1)}, f32[136,512]{1,0:T(8,128)S(1)}) custom-call(s32[4]{0:T(128)S(1)} %pad_add_fusion.meta, s32[2,80]{1,0:T(2,128)S(1)} %get-tuple-element.11.plan, bf16[128,1024]{1,0:T(8,128)(2,1)S(1)} %collective-permute-done.6.q_ref, bf16[4096,1024]{1,0:T(8,128)(2,1)S(1)} %get-tuple-element.12.rows_ref), custom_call_target="tpu_custom_call" | custom-call | flops 1073741824 | bytes 1048576 | tf_op jit(solution)/shard_map/block1/pallas_call | solution.py:118
  22.7 0.1 collective-permute-start.7
  22.8 0.7 %collective-permute-done.3 = f16[136,512]{1,0:T(8,128)(2,1)S(1)} collective-permute-done((f16[136,512]{1,0:T(8,128)(2,1)S(1)}, f16[136,512]{1,0:T(8,128)(2,1)S(1)}, u32[]{:S(2)}, u32[]{:S(2)}) %collective-permute-start.3) | collective-permute-done | bytes 139296 | tf_op jit(solution)/shard_map/ppermute | solution.py:159
  23.6 2.7 %collective-permute-start.4 = (f16[136,256]{1,0:T(8,128)(2,1)S(1)}, f16[136,256]{1,0:T(8,128)(2,1)S(1)}, u32[]{:S(2)}, u32[]{:S(2)}) collective-permute-start(f16[136,256]{1,0:T(8,128)(2,1)S(1)} %get-tuple-element.17), channel_id=1, source_target_pairs={{0,0},{1,5},{2,2},{3,7},{4,4},{5,1},{6,6},{7,3},{8,8},{9,13},{10,1... | collective-permute-start | bytes 208904 | tf_op jit(solution)/shard_map/ppermute | solution.py:167
  26.3 0.1 collective-permute-start.5
  26.4 1.2 %collective-permute-done.7 = f16[136,512]{1,0:T(8,128)(2,1)S(1)} collective-permute-done((f16[136,512]{1,0:T(8,128)(2,1)S(1)}, f16[136,512]{1,0:T(8,128)(2,1)S(1)}, u32[]{:S(2)}, u32[]{:S(2)}) %collective-permute-start.7) | collective-permute-done | bytes 139296 | tf_op jit(solution)/shard_map/ppermute | solution.py:160
  27.6 1.7 %collective-permute-start.8 = (f16[136,256]{1,0:T(8,128)(2,1)S(1)}, f16[136,256]{1,0:T(8,128)(2,1)S(1)}, u32[]{:S(2)}, u32[]{:S(2)}) collective-permute-start(f16[136,256]{1,0:T(8,128)(2,1)S(1)} %get-tuple-element.19), channel_id=1, source_target_pairs={{0,8},{1,13},{2,10},{3,15},{4,12},{5,9},{6,14},{7,11},{8,0},{9,5},... | collective-permute-start | bytes 208904 | tf_op jit(solution)/shard_map/ppermute | solution.py:165
  29.4 2.1 %collective-permute-start.9 = (f16[136,256]{1,0:T(8,128)(2,1)S(1)}, f16[136,256]{1,0:T(8,128)(2,1)S(1)}, u32[]{:S(2)}, u32[]{:S(2)}) collective-permute-start(f16[136,256]{1,0:T(8,128)(2,1)S(1)} %get-tuple-element.20), channel_id=1, source_target_pairs={{0,9},{1,12},{2,11},{3,14},{4,13},{5,8},{6,15},{7,10},{8,1},{9,4},... | collective-permute-start | bytes 208904 | tf_op jit(solution)/shard_map/ppermute | solution.py:166
  31.5 0.0 collective-permute-done.4
  31.5 0.0 collective-permute-done.5
  31.5 1.2 %collective-permute-done.8 = f16[136,256]{1,0:T(8,128)(2,1)S(1)} collective-permute-done((f16[136,256]{1,0:T(8,128)(2,1)S(1)}, f16[136,256]{1,0:T(8,128)(2,1)S(1)}, u32[]{:S(2)}, u32[]{:S(2)}) %collective-permute-start.8) | collective-permute-done | bytes 69664 | tf_op jit(solution)/shard_map/ppermute | solution.py:165
  32.7 4.5 %collective-permute-done.9 = f16[136,256]{1,0:T(8,128)(2,1)S(1)} collective-permute-done((f16[136,256]{1,0:T(8,128)(2,1)S(1)}, f16[136,256]{1,0:T(8,128)(2,1)S(1)}, u32[]{:S(2)}, u32[]{:S(2)}) %collective-permute-start.9) | collective-permute-done | bytes 69664 | tf_op jit(solution)/shard_map/ppermute | solution.py:166
  37.2 1.6 %fusion = f32[128,256]{1,0:T(8,128)} fusion(f32[136,256]{1,0:T(8,128)S(1)} %add_add_fusion, f32[128]{0:T(128)S(1)} %fusion.2, bf16[128,1024]{1,0:T(8,128)(2,1)} %param.5, s32[]{:T(128)S(6)} %select_n.18), kind=kLoop, calls=%fused_computation.4 | loop fusion | flops 98304 | bytes 328196 | tf_op jit(solution)/shard_map/add | solution.py:173
  (8 shorter events, 0.2 us)
Async XLA Ops:
  0.0 9.4 %collective-permute-start.1 = (bf16[2048,1024]{1,0:T(8,128)(2,1)}, bf16[2048,1024]{1,0:T(8,128)(2,1)}, u32[]{:S(2)}, u32[]{:S(2)}) collective-permute-start(bf16[2048,1024]{1,0:T(8,128)(2,1)} %db_ref.1), channel_id=1, source_target_pairs={{0,1},{1,0},{2,3},{3,2},{4,5},{5,4},{6,7},{7,6},{8,9},{9,8},{10,11... | collective-permute-start | bytes 12582920 | tf_op jit(solution)/shard_map/ppermute | solution.py:150
  0.1 15.2 %collective-permute-start.2 = (bf16[128,1024]{1,0:T(8,128)(2,1)}, bf16[128,1024]{1,0:T(8,128)(2,1)S(1)}, u32[]{:S(2)}, u32[]{:S(2)}) collective-permute-start(bf16[128,1024]{1,0:T(8,128)(2,1)} %param.5), channel_id=1, source_target_pairs={{0,0},{1,5},{2,2},{3,7},{4,4},{5,1},{6,6},{7,3},{8,8},{9,13},{10,1... | collective-permute-start | bytes 786440 | tf_op jit(solution)/shard_map/ppermute | solution.py:152
  4.7 15.0 %collective-permute-start.6 = (bf16[128,1024]{1,0:T(8,128)(2,1)}, bf16[128,1024]{1,0:T(8,128)(2,1)S(1)}, u32[]{:S(2)}, u32[]{:S(2)}) collective-permute-start(bf16[128,1024]{1,0:T(8,128)(2,1)} %param.5), channel_id=1, source_target_pairs={{0,8},{1,13},{2,10},{3,15},{4,12},{5,9},{6,14},{7,11},{8,0},{9,5},... | collective-permute-start | bytes 786440 | tf_op jit(solution)/shard_map/ppermute | solution.py:151
  8.3 1.1 %collective-permute-start = (s32[1,32]{1,0:T(1,128)S(1)}, s32[1,32]{1,0:T(1,128)S(1)}, u32[]{:S(2)}, u32[]{:S(2)}) collective-permute-start(s32[1,32]{1,0:T(1,128)S(1)} %compare_select_fusion.own_code), channel_id=1, source_target_pairs={{0,1},{1,0},{2,3},{3,2},{4,5},{5,4},{6,7},{7,6},{8,9},{9,8},{10,11... | collective-permute-start | bytes 392 | tf_op jit(solution)/shard_map/ppermute | solution.py:153
  9.4 2.2 %copy-start = (bf16[2048,1024]{1,0:T(8,128)(2,1)S(1)}, bf16[2048,1024]{1,0:T(8,128)(2,1)}, u32[]{:S(2)}) copy-start(bf16[2048,1024]{1,0:T(8,128)(2,1)} %db_ref.1) | copy-start | bytes 12582916
  18.4 5.1 %collective-permute-start.3 = (f16[136,512]{1,0:T(8,128)(2,1)S(1)}, f16[136,512]{1,0:T(8,128)(2,1)S(1)}, u32[]{:S(2)}, u32[]{:S(2)}) collective-permute-start(f16[136,512]{1,0:T(8,128)(2,1)S(1)} %convert_element_type.34), channel_id=1, source_target_pairs={{0,2},{1,3},{2,0},{3,1},{4,6},{5,7},{6,4},{7,5},{8,10},{9,11},{10,... | collective-permute-start | bytes 417800 | tf_op jit(solution)/shard_map/ppermute | solution.py:159
  22.7 4.8 %collective-permute-start.7 = (f16[136,512]{1,0:T(8,128)(2,1)S(1)}, f16[136,512]{1,0:T(8,128)(2,1)S(1)}, u32[]{:S(2)}, u32[]{:S(2)}) collective-permute-start(f16[136,512]{1,0:T(8,128)(2,1)S(1)} %convert_element_type.39), channel_id=1, source_target_pairs={{0,2},{1,3},{2,0},{3,1},{4,6},{5,7},{6,4},{7,5},{8,10},{9,11},{10,... | collective-permute-start | bytes 417800 | tf_op jit(solution)/shard_map/ppermute | solution.py:160
  23.6 7.9 %collective-permute-start.4 = (f16[136,256]{1,0:T(8,128)(2,1)S(1)}, f16[136,256]{1,0:T(8,128)(2,1)S(1)}, u32[]{:S(2)}, u32[]{:S(2)}) collective-permute-start(f16[136,256]{1,0:T(8,128)(2,1)S(1)} %get-tuple-element.17), channel_id=1, source_target_pairs={{0,0},{1,5},{2,2},{3,7},{4,4},{5,1},{6,6},{7,3},{8,8},{9,13},{10,1... | collective-permute-start | bytes 208904 | tf_op jit(solution)/shard_map/ppermute | solution.py:167
  26.3 5.2 %collective-permute-start.5 = (f16[136,256]{1,0:T(8,128)(2,1)S(1)}, f16[136,256]{1,0:T(8,128)(2,1)S(1)}, u32[]{:S(2)}, u32[]{:S(2)}) collective-permute-start(f16[136,256]{1,0:T(8,128)(2,1)S(1)} %get-tuple-element.18), channel_id=1, source_target_pairs={{0,1},{1,4},{2,3},{3,6},{4,5},{5,0},{6,7},{7,2},{8,9},{9,12},{10,1... | collective-permute-start | bytes 208904 | tf_op jit(solution)/shard_map/ppermute | solution.py:168
  27.6 5.0 %collective-permute-start.8 = (f16[136,256]{1,0:T(8,128)(2,1)S(1)}, f16[136,256]{1,0:T(8,128)(2,1)S(1)}, u32[]{:S(2)}, u32[]{:S(2)}) collective-permute-start(f16[136,256]{1,0:T(8,128)(2,1)S(1)} %get-tuple-element.19), channel_id=1, source_target_pairs={{0,8},{1,13},{2,10},{3,15},{4,12},{5,9},{6,14},{7,11},{8,0},{9,5},... | collective-permute-start | bytes 208904 | tf_op jit(solution)/shard_map/ppermute | solution.py:165
  29.4 7.8 %collective-permute-start.9 = (f16[136,256]{1,0:T(8,128)(2,1)S(1)}, f16[136,256]{1,0:T(8,128)(2,1)S(1)}, u32[]{:S(2)}, u32[]{:S(2)}) collective-permute-start(f16[136,256]{1,0:T(8,128)(2,1)S(1)} %get-tuple-element.20), channel_id=1, source_target_pairs={{0,9},{1,12},{2,11},{3,14},{4,13},{5,8},{6,15},{7,10},{8,1},{9,4},... | collective-permute-start | bytes 208904 | tf_op jit(solution)/shard_map/ppermute | solution.py:166

commit v3 on v2

v3 whole, which is shorter than its diff:
```python
import functools
import math

import jax
import jax.numpy as jnp
from jax import lax
from jax.experimental import pallas as pl
from jax.experimental.pallas import tpu as pltpu
from jax.sharding import PartitionSpec as P

BLK = 128
EXTRA = 8
score_gain = 2.0
WIRE = jnp.float16
SMEM = pl.BlockSpec(memory_space=pltpu.SMEM)
VMEM = pl.BlockSpec(memory_space=pltpu.VMEM)
HBM = pl.BlockSpec(memory_space=pltpu.MemorySpace.HBM)
GROUP = 8


def plan_kernel(blocks, meta, own_code, other_code, plan_ref):
    last = plan_ref.shape[1] - 1
    counts = [jnp.int32(0), jnp.int32(0)]
    for code_ref, base in ((own_code, 0), (other_code, blocks)):
        for j in range(code_ref.shape[1]):
            code = code_ref[0, j]
            for which in range(2):
                plan_ref[which, counts[which]] = base + (code & 255)
                counts[which] = counts[which] + ((code >> 8) == meta[which]).astype(jnp.int32)
    for which in range(2):
        n = counts[which]
        final = jnp.where(n > 0, plan_ref[which, jnp.maximum(n - 1, 0)], 0)
        for i in range(GROUP):
            plan_ref[which, n + i] = final
        plan_ref[which, last] = n


def make_plan(meta, own_code, other_code, blocks):
    slots = own_code.shape[1]
    return pl.pallas_call(
        functools.partial(plan_kernel, blocks),
        out_shape=jax.ShapeDtypeStruct((2, 2 * slots + 16), jnp.int32),
        in_specs=[SMEM, SMEM, SMEM],
        out_specs=SMEM,
        compiler_params=pltpu.CompilerParams(vmem_limit_bytes=1024 * 1024),
        name="plan",
    )(meta, own_code, other_code)


def block_kernel(scale, which, meta, plan, q_ref, *refs):
    side, core = meta[2], meta[3]
    n = plan[which, plan.shape[1] - 1]
    size = GROUP if which else GROUP // 2
    half_group = GROUP // 2
    if which == 0:
        mine_ref, own_ref, other_ref, send_ref, keep_ref, next_ref, cut_ref, acc, wacc, rows_ref, sems, next_sems, cut_sem = refs
        shard_blocks = own_ref.shape[0] // BLK

        def copy(ref, at, to_ref, i, sem):
            start = pl.multiple_of(at * BLK, BLK)
            to = pl.multiple_of(i * BLK, BLK)
            return pltpu.make_async_copy(ref.at[pl.ds(start, BLK)], to_ref.at[pl.ds(to, BLK)], sem.at[i])

        def fetch(listing, to_ref, sem):
            def issue(i, carry):
                at = plan[listing, i]

                @pl.when(at < shard_blocks)
                def _():
                    copy(own_ref, at, to_ref, i, sem).start()

                @pl.when(at >= shard_blocks)
                def _():
                    copy(other_ref, at - shard_blocks, to_ref, i, sem).start()
                return carry
            count = (plan[listing, plan.shape[1] - 1] + half_group - 1) // half_group * half_group
            lax.fori_loop(0, count, issue, 0)
            return count

        cut = cut_ref.shape[1]
        start = pl.multiple_of((2 * side + core) * cut, cut)
        trim = pltpu.make_async_copy(mine_ref.at[:, pl.ds(start, cut)], cut_ref, cut_sem)
        fetch(0, rows_ref, sems)
        coming = fetch(1, next_ref, next_sems)
        trim.start()
    else:
        rows_ref, send_ref, keep_ref, acc, wacc = refs
    acc[...] = jnp.zeros_like(acc)
    wacc[...] = jnp.zeros_like(wacc)

    def visit(first, group):
        if which == 0:
            for g in range(group):
                copy(own_ref, 0, rows_ref, first + g, sems).wait()
        tile = rows_ref[pl.ds(pl.multiple_of(first * BLK, half_group * BLK), group * BLK), :]
        s = lax.dot_general(q_ref[...], tile, (((1,), (1,)), ((), ())), preferred_element_type=jnp.float32)
        w = 0.5 * jnp.tanh(s * (0.5 * scale)) + 0.5
        col = lax.broadcasted_iota(jnp.int32, w.shape, 1)
        w = jnp.where(col < (n - first) * BLK, w, 0.0)
        wsum = wacc[...]
        for g in range(group):
            wsum = wsum + w[:, g * BLK:(g + 1) * BLK]
        wacc[...] = wsum
        acc[...] += jnp.dot(w.astype(jnp.bfloat16), tile, preferred_element_type=jnp.float32)

    wide = (n + half_group - 1) // size

    def step(i, carry):
        visit(size * i, size)
        return carry

    lax.fori_loop(0, wide, step, 0)

    if size > half_group:
        @pl.when(size * wide < n)
        def _():
            visit(size * wide, half_group)

    half = send_ref.shape[1]
    piece = half // 2
    totals = jnp.sum(jnp.transpose(wacc[...]), axis=0, keepdims=True)
    totals = jnp.broadcast_to(totals, (EXTRA, BLK))
    totals = jnp.concatenate([totals] * (piece // BLK), axis=1)
    for ref, x in ((send_ref, 1 - side), (keep_ref, side)):
        for p, c in ((0, core), (1, 1 - core)):
            start = pl.multiple_of(x * half + c * piece, piece)
            ref[pl.ds(0, BLK), pl.ds(p * piece, piece)] = acc[:, pl.ds(start, piece)]
            ref[pl.ds(BLK, EXTRA), pl.ds(p * piece, piece)] = totals
    if which == 0:
        trim.wait()

        def settle(i, carry):
            copy(own_ref, 0, next_ref, i, next_sems).wait()
            return carry
        lax.fori_loop(0, coming, settle, 0)


def block_sums(which, meta, plan, q, *sources):
    width = q.shape[1]
    scale = score_gain / math.sqrt(width)
    half = jax.ShapeDtypeStruct((BLK + EXTRA, width // 2), jnp.float32)
    outs = [half, half]
    scratch = [pltpu.VMEM((BLK, width), jnp.float32), pltpu.VMEM((BLK, BLK), jnp.float32)]
    if which == 0:
        most = 2 * sources[1].shape[0]
        outs.append(jax.ShapeDtypeStruct((most, width), q.dtype))
        outs.append(jax.ShapeDtypeStruct((BLK, width // 4), q.dtype))
        scratch += [pltpu.VMEM((most, width), q.dtype)] + [pltpu.SemaphoreType.DMA((most // BLK,))] * 2
        scratch.append(pltpu.SemaphoreType.DMA)
    return pl.pallas_call(
        functools.partial(block_kernel, scale, which),
        out_shape=outs,
        in_specs=[SMEM, SMEM, VMEM] + [HBM if which == 0 else VMEM] * len(sources),
        out_specs=[VMEM] * len(outs),
        scratch_shapes=scratch,
        compiler_params=pltpu.CompilerParams(vmem_limit_bytes=(20 if which == 0 else 8) * 1024 * 1024),
        name=f"block{which}",
    )(meta, plan, q, *sources)


def paired(queries, database, pair_query, pair_db, pair_count):
    width = queries.shape[1]
    z = lax.axis_index("db")
    place = lax.axis_index("loop")
    side, core = place // 2, place % 2
    both = ("db", "loop")
    grid = [(i, j) for i in range(4) for j in range(4)]
    core_swap = [(j, j ^ 1) for j in range(4)]
    side_swap = [(j, j ^ 2) for j in range(4)]

    def hop(base, turn):
        return [(4 * i + j, 4 * (i ^ (base + (j & 1))) + (j ^ turn)) for i, j in grid]

    slot = lax.broadcasted_iota(jnp.int32, pair_query.shape, 1)
    code = jnp.where(slot < pair_count[0], pair_query * 256 + pair_db, -256)
    other_code = lax.ppermute(code, "loop", core_swap)
    other = lax.ppermute(database, "loop", core_swap)
    second = lax.ppermute(queries, both, hop(2, 0))
    first = lax.ppermute(queries, both, hop(0, 0))
    meta = jnp.stack([z ^ core, z ^ core ^ 2, side, core]).astype(jnp.int32)
    plan = make_plan(meta, code, other_code, database.shape[0] // BLK)
    away = pltpu.MemorySpace.HBM
    send1, keep1, rows, own = block_sums(
        0, meta, plan, first, pltpu.with_memory_space_constraint(queries, away),
        pltpu.with_memory_space_constraint(database, away),
        pltpu.with_memory_space_constraint(other, away))
    send2, keep2 = block_sums(1, meta, plan, second, rows)
    got1 = lax.ppermute(send1.astype(WIRE), "loop", side_swap)
    got2 = lax.ppermute(send2.astype(WIRE), "loop", side_swap)
    piece = width // 4

    def pass_on(keep, got, turn, base):
        lanes = slice(turn * piece, (turn + 1) * piece)
        summed = (keep[:, lanes] + got[:, lanes].astype(jnp.float32)).astype(WIRE)
        return lax.ppermute(summed, both, hop(base, turn))

    parts = [
        pass_on(keep2, got2, 0, 2),
        pass_on(keep2, got2, 1, 2),
        pass_on(keep1, got1, 0, 0),
        pass_on(keep1, got1, 1, 0),
    ]
    parts = [p.astype(jnp.float32) for p in parts]
    total = (parts[2] + parts[3]) + (parts[0] + parts[1])
    return own.astype(jnp.float32) + total[:BLK] * lax.rsqrt(1.0 + total[BLK, :BLK])[:, None]


def per_device(queries, database, pair_query, pair_db, pair_count):
    if lax.axis_size("db") == 4 and lax.axis_size("loop") == 4 and queries.shape[0] == BLK:
        return paired(queries, database, pair_query, pair_db, pair_count)
    panels = lax.all_gather(queries, "db", axis=0, tiled=True)
    query_rows, feature_count = panels.shape
    score_scale = score_gain / math.sqrt(feature_count)
    slot_query, slot_db, live_count = pair_query[0], pair_db[0], pair_count[0]

    def visit(slot_no, state_pair):
        summed, totals = state_pair
        query_start = slot_query[slot_no] * BLK
        query_tile = lax.dynamic_slice_in_dim(panels, query_start, BLK, 0)
        db_tile = lax.dynamic_slice_in_dim(database, slot_db[slot_no] * BLK, BLK, 0)
        scores = lax.dot_general(
            query_tile, db_tile, (((1,), (1,)), ((), ())), preferred_element_type=jnp.float32
        ) * score_scale
        weights = jax.nn.sigmoid(scores)
        contrib = jnp.dot(weights.astype(jnp.bfloat16), db_tile, preferred_element_type=jnp.float32)
        old_rows = lax.dynamic_slice_in_dim(summed, query_start, BLK, 0)
        summed = lax.dynamic_update_slice_in_dim(summed, old_rows + contrib, query_start, 0)
        old_totals = lax.dynamic_slice_in_dim(totals, query_start, BLK, 0)
        totals = lax.dynamic_update_slice_in_dim(
            totals, old_totals + jnp.sum(weights, axis=1, keepdims=True), query_start, 0
        )
        return (summed, totals)

    start = (
        jnp.zeros((query_rows, feature_count), jnp.float32),
        jnp.zeros((query_rows, 1), jnp.float32),
    )
    summed_rows, total_rows = lax.fori_loop(0, live_count, visit, start)
    column_width = feature_count // lax.axis_size("loop")
    own_profiles = lax.dynamic_slice_in_dim(
        queries, lax.axis_index("loop") * column_width, column_width, 1
    ).astype(jnp.float32)
    row_sums = lax.psum_scatter(summed_rows, "db", scatter_dimension=0, tiled=True)
    row_weights = lax.psum_scatter(total_rows, "db", scatter_dimension=0, tiled=True)
    partial_out = lax.psum_scatter(row_sums, "loop", scatter_dimension=1, tiled=True)
    weight_out = lax.psum(row_weights, "loop")
    return own_profiles + partial_out * lax.rsqrt(1.0 + weight_out)


def solution(mesh):
    return jax.shard_map(
        per_device,
        mesh=mesh,
        in_specs=(
            P(("parts", "db"), None),
            P(("parts", "db", "loop"), None),
            P(("parts", "db", "loop"), None),
            P(("parts", "db", "loop"), None),
            P(("parts", "db", "loop")),
        ),
        out_specs=P(("parts", "db"), "loop"),
        check_vma=False,
    )
```

time: 39.3 us -> 37.1 us (0.944)
  starting transfers between devices: 15 us -> 19.6 us
  Pallas kernels: 9.72 us -> 7.42 us
  local copies, waits for them, and re-layouts: 2.24 us -> 0 us
  waiting for transfers between devices: 8.56 us -> 7.06 us
  other arithmetic: 2.53 us -> 1.67 us
    pallas_call x3, Pallas kernels: 9.72 us -> 7.42 us  [the longest x2 5.89 us: block_sums(): pl.pallas_call(functools.partial(block_kernel, scale, which), out_shape=o...]
    ppermute x4, starting transfers between devices: 6.66 us -> 8.91 us  [pass_on(): return lax.ppermute(summed, both, hop(base, turn))]
    unnamed x2 -> x0, local copies, waits for them, and re-layouts: 2.19 us -> none
    ppermute x1, starting transfers between devices: 1.29 us -> 2.85 us  [paired(): got1 = lax.ppermute(send1.astype(WIRE), 'loop', side_swap)]
    ppermute x1, waiting for transfers between devices: 1.15 us -> 0.01 us  [paired(): got2 = lax.ppermute(send2.astype(WIRE), 'loop', side_swap)]
    add x1, other arithmetic: 1.59 us -> 0.74 us  [paired(): own.astype(jnp.float32)]
    ppermute x4, waiting for transfers between devices: 5.66 us -> 4.82 us  [pass_on(): return lax.ppermute(summed, both, hop(base, turn))]
    ppermute x1, starting transfers between devices: 0.07 us -> 0.86 us  [paired(): got2 = lax.ppermute(send2.astype(WIRE), 'loop', side_swap)]
  transfers between devices with their start and end apart: 10 -> 10, of which waited for: 5 -> 3; matrix products, arithmetic and copies ran while one was open for 2% -> 2% of each run, Pallas kernels for 25% -> 20%
where the time goes in v3:
time: 37.1 us; the launch traced here: 36.5 us
  starting transfers between devices  19.6 us (53%)
  Pallas kernels  7.42 us (20%)
  waiting for transfers between devices  7.06 us (19%)
  other arithmetic  1.67 us (5%)
  between operations  0.76 us (2%)
    ppermute x4, starting transfers between devices, pass_on(): return lax.ppermute(summed, both, hop(base, turn))  8.91 us
    pallas_call x2, Pallas kernels, block_sums(): pl.pallas_call(functools.partial(block_kernel, scale, which), out_shape=o...  5.89 us
    ppermute x4, waiting for transfers between devices, pass_on(): return lax.ppermute(summed, both, hop(base, turn))  4.82 us
    ppermute x1, starting transfers between devices, paired(): first = lax.ppermute(queries, both, hop(0, 0))  4.64 us
    ppermute x1, starting transfers between devices, paired(): got1 = lax.ppermute(send1.astype(WIRE), 'loop', side_swap)  2.85 us
    ppermute x1, starting transfers between devices, paired(): second = lax.ppermute(queries, both, hop(2, 0))  2.26 us
    pallas_call x1, Pallas kernels, make_plan(): pl.pallas_call(functools.partial(plan_kernel, blocks), out_shape=jax.Shap...  1.53 us
    ppermute x1, waiting for transfers between devices, paired(): got1 = lax.ppermute(send1.astype(WIRE), 'loop', side_swap)  1.18 us
  transfers between devices with their start and end apart: 10, of which 3 were waited for; matrix products, arithmetic and copies ran while one was open for 2% of the time, Pallas kernels for 20%

profile of v3, /device:TPU:1, one launch (start us, length us, event | category | flops | bytes accessed | tf_op | source)
XLA Modules:
  0.0 36.5 jit_solution(14824627283231349932)
XLA Ops:
  0.0 0.1 collective-permute-start.2
  0.1 4.6 %collective-permute-start.1 = (bf16[128,1024]{1,0:T(8,128)(2,1)}, bf16[128,1024]{1,0:T(8,128)(2,1)S(1)}, u32[]{:S(2)}, u32[]{:S(2)}) collective-permute-start(bf16[128,1024]{1,0:T(8,128)(2,1)} %refs_0_.1), channel_id=1, source_target_pairs={{0,0},{1,5},{2,2},{3,7},{4,4},{5,1},{6,6},{7,3},{8,8},{9,13},{10,1... | collective-permute-start | bytes 786440 | tf_op jit(solution)/shard_map/ppermute | solution.py:179
  4.7 2.3 %collective-permute-start.6 = (bf16[128,1024]{1,0:T(8,128)(2,1)}, bf16[128,1024]{1,0:T(8,128)(2,1)S(1)}, u32[]{:S(2)}, u32[]{:S(2)}) collective-permute-start(bf16[128,1024]{1,0:T(8,128)(2,1)} %refs_0_.1), channel_id=1, source_target_pairs={{0,8},{1,13},{2,10},{3,15},{4,12},{5,9},{6,14},{7,11},{8,0},{9,5},... | collective-permute-start | bytes 786440 | tf_op jit(solution)/shard_map/ppermute | solution.py:178
  7.6 0.7 %compare_select_fusion.own_code = s32[1,32]{1,0:T(1,128)S(1)} fusion(s32[1,32]{1,0:T(1,128)} %param.8, s32[1,32]{1,0:T(1,128)} %param.7, s32[]{:T(128)} %bitcast.7), kind=kLoop, calls=%fused_computation.7 | loop fusion | flops 128 | bytes 388 | tf_op jit(solution)/shard_map/jit(_where)/select_n | solution.py:175
  8.3 0.0 collective-permute-start
  8.3 0.1 pad_add_fusion.meta
  8.4 1.0 %collective-permute-done.other_code = s32[1,32]{1,0:T(1,128)S(1)} collective-permute-done((s32[1,32]{1,0:T(1,128)S(1)}, s32[1,32]{1,0:T(1,128)S(1)}, u32[]{:S(2)}, u32[]{:S(2)}) %collective-permute-start) | collective-permute-done | bytes 160 | tf_op jit(solution)/shard_map/ppermute | solution.py:176
  9.4 1.5 %plan.1 = s32[2,80]{1,0:T(2,128)S(1)} custom-call(s32[4]{0:T(128)S(1)} %pad_add_fusion.meta, s32[1,32]{1,0:T(1,128)S(1)} %compare_select_fusion.own_code, s32[1,32]{1,0:T(1,128)S(1)} %collective-permute-done.other_code), custom_call_target="tpu_custom_call" | custom-call | tf_op jit(solution)/shard_map/plan/pallas_call | solution.py:40
  11.0 0.0 collective-permute-done.1.q_ref
  11.0 0.0 collective-permute-done.2.refs_2_
  11.0 4.0 %block0.1 = (f32[136,512]{1,0:T(8,128)S(1)}, f32[136,512]{1,0:T(8,128)S(1)}, bf16[4096,1024]{1,0:T(8,128)(2,1)S(1)}, bf16[128,256]{1,0:T(8,128)(2,1)S(1)}) custom-call(s32[4]{0:T(128)S(1)} %pad_add_fusion.meta, s32[2,80]{1,0:T(2,128)S(1)} %plan.1, bf16[128,1024]{1,0:T(8,128)(2,1)S(1)} %collective-permute-done.1.q_ref, bf16[128,1024]{1,0:T(8,128)(2,1)} %refs_0_.1, ...), custom_call_target="tpu_custom_call" | custom-call | tf_op jit(solution)/shard_map/block0/pallas_call | solution.py:150
  15.0 2.8 %collective-permute-start.3 = (f16[136,512]{1,0:T(8,128)(2,1)S(1)}, f16[136,512]{1,0:T(8,128)(2,1)S(1)}, u32[]{:S(2)}, u32[]{:S(2)}) collective-permute-start(f16[136,512]{1,0:T(8,128)(2,1)S(1)} %convert_element_type.46), channel_id=1, source_target_pairs={{0,2},{1,3},{2,0},{3,1},{4,6},{5,7},{6,4},{7,5},{8,10},{9,11},{10,... | collective-permute-start | bytes 417800 | tf_op jit(solution)/shard_map/ppermute | solution.py:188
  17.9 0.0 collective-permute-done.6.q_ref
  17.9 1.9 %block1.1 = (f32[136,512]{1,0:T(8,128)S(1)}, f32[136,512]{1,0:T(8,128)S(1)}) custom-call(s32[4]{0:T(128)S(1)} %pad_add_fusion.meta, s32[2,80]{1,0:T(2,128)S(1)} %plan.1, bf16[128,1024]{1,0:T(8,128)(2,1)S(1)} %collective-permute-done.6.q_ref, bf16[4096,1024]{1,0:T(8,128)(2,1)S(1)} %get-tuple-element.14.refs_0_), custom_call_target="tpu_custom_call" | custom-call | tf_op jit(solution)/shard_map/block1/pallas_call | solution.py:150
  19.8 0.9 %collective-permute-start.7 = (f16[136,512]{1,0:T(8,128)(2,1)S(1)}, f16[136,512]{1,0:T(8,128)(2,1)S(1)}, u32[]{:S(2)}, u32[]{:S(2)}) collective-permute-start(f16[136,512]{1,0:T(8,128)(2,1)S(1)} %convert_element_type.53), channel_id=1, source_target_pairs={{0,2},{1,3},{2,0},{3,1},{4,6},{5,7},{6,4},{7,5},{8,10},{9,11},{10,... | collective-permute-start | bytes 417800 | tf_op jit(solution)/shard_map/ppermute | solution.py:189
  20.6 1.2 %collective-permute-done.3 = f16[136,512]{1,0:T(8,128)(2,1)S(1)} collective-permute-done((f16[136,512]{1,0:T(8,128)(2,1)S(1)}, f16[136,512]{1,0:T(8,128)(2,1)S(1)}, u32[]{:S(2)}, u32[]{:S(2)}) %collective-permute-start.3) | collective-permute-done | bytes 139296 | tf_op jit(solution)/shard_map/ppermute | solution.py:188
  21.9 3.5 %collective-permute-start.4 = (f16[136,256]{1,0:T(8,128)(2,1)S(1)}, f16[136,256]{1,0:T(8,128)(2,1)S(1)}, u32[]{:S(2)}, u32[]{:S(2)}) collective-permute-start(f16[136,256]{1,0:T(8,128)(2,1)S(1)} %get-tuple-element.17), channel_id=1, source_target_pairs={{0,0},{1,5},{2,2},{3,7},{4,4},{5,1},{6,6},{7,3},{8,8},{9,13},{10,1... | collective-permute-start | bytes 208904 | tf_op jit(solution)/shard_map/ppermute | solution.py:195
  25.4 0.1 collective-permute-start.5
  25.5 0.0 collective-permute-done.7
  25.5 2.0 %collective-permute-start.8 = (f16[136,256]{1,0:T(8,128)(2,1)S(1)}, f16[136,256]{1,0:T(8,128)(2,1)S(1)}, u32[]{:S(2)}, u32[]{:S(2)}) collective-permute-start(f16[136,256]{1,0:T(8,128)(2,1)S(1)} %get-tuple-element.19), channel_id=1, source_target_pairs={{0,8},{1,13},{2,10},{3,15},{4,12},{5,9},{6,14},{7,11},{8,0},{9,5},... | collective-permute-start | bytes 208904 | tf_op jit(solution)/shard_map/ppermute | solution.py:195
  27.5 3.3 %collective-permute-start.9 = (f16[136,256]{1,0:T(8,128)(2,1)S(1)}, f16[136,256]{1,0:T(8,128)(2,1)S(1)}, u32[]{:S(2)}, u32[]{:S(2)}) collective-permute-start(f16[136,256]{1,0:T(8,128)(2,1)S(1)} %get-tuple-element.20), channel_id=1, source_target_pairs={{0,9},{1,12},{2,11},{3,14},{4,13},{5,8},{6,15},{7,10},{8,1},{9,4},... | collective-permute-start | bytes 208904 | tf_op jit(solution)/shard_map/ppermute | solution.py:195
  30.9 0.0 collective-permute-done.4
  30.9 0.0 collective-permute-done.5
  30.9 0.0 collective-permute-done.8
  30.9 4.8 %collective-permute-done.9 = f16[136,256]{1,0:T(8,128)(2,1)S(1)} collective-permute-done((f16[136,256]{1,0:T(8,128)(2,1)S(1)}, f16[136,256]{1,0:T(8,128)(2,1)S(1)}, u32[]{:S(2)}, u32[]{:S(2)}) %collective-permute-start.9) | collective-permute-done | bytes 69664 | tf_op jit(solution)/shard_map/ppermute | solution.py:195
  35.7 0.7 %fusion = f32[128,256]{1,0:T(8,128)} fusion(f32[136,256]{1,0:T(8,128)S(1)} %add_add_fusion, bf16[128,256]{1,0:T(8,128)(2,1)S(1)} %get-tuple-element.11, f32[128]{0:T(128)S(1)} %fusion.2), kind=kLoop, calls=%fused_computation.6 | loop fusion | flops 98304 | bytes 328192 | tf_op jit(solution)/shard_map/add | solution.py:205
  (6 shorter events, 0.2 us)
Async XLA Ops:
  0.0 11.0 %collective-permute-start.2 = (bf16[2048,1024]{1,0:T(8,128)(2,1)}, bf16[2048,1024]{1,0:T(8,128)(2,1)}, u32[]{:S(2)}, u32[]{:S(2)}) collective-permute-start(bf16[2048,1024]{1,0:T(8,128)(2,1)} %refs_1_.1), channel_id=1, source_target_pairs={{0,1},{1,0},{2,3},{3,2},{4,5},{5,4},{6,7},{7,6},{8,9},{9,8},{10,11... | collective-permute-start | bytes 12582920 | tf_op jit(solution)/shard_map/ppermute | solution.py:177
  0.1 10.9 %collective-permute-start.1 = (bf16[128,1024]{1,0:T(8,128)(2,1)}, bf16[128,1024]{1,0:T(8,128)(2,1)S(1)}, u32[]{:S(2)}, u32[]{:S(2)}) collective-permute-start(bf16[128,1024]{1,0:T(8,128)(2,1)} %refs_0_.1), channel_id=1, source_target_pairs={{0,0},{1,5},{2,2},{3,7},{4,4},{5,1},{6,6},{7,3},{8,8},{9,13},{10,1... | collective-permute-start | bytes 786440 | tf_op jit(solution)/shard_map/ppermute | solution.py:179
  4.7 13.2 %collective-permute-start.6 = (bf16[128,1024]{1,0:T(8,128)(2,1)}, bf16[128,1024]{1,0:T(8,128)(2,1)S(1)}, u32[]{:S(2)}, u32[]{:S(2)}) collective-permute-start(bf16[128,1024]{1,0:T(8,128)(2,1)} %refs_0_.1), channel_id=1, source_target_pairs={{0,8},{1,13},{2,10},{3,15},{4,12},{5,9},{6,14},{7,11},{8,0},{9,5},... | collective-permute-start | bytes 786440 | tf_op jit(solution)/shard_map/ppermute | solution.py:178
  8.3 1.1 %collective-permute-start = (s32[1,32]{1,0:T(1,128)S(1)}, s32[1,32]{1,0:T(1,128)S(1)}, u32[]{:S(2)}, u32[]{:S(2)}) collective-permute-start(s32[1,32]{1,0:T(1,128)S(1)} %compare_select_fusion.own_code), channel_id=1, source_target_pairs={{0,1},{1,0},{2,3},{3,2},{4,5},{5,4},{6,7},{7,6},{8,9},{9,8},{10,11... | collective-permute-start | bytes 392 | tf_op jit(solution)/shard_map/ppermute | solution.py:176
  15.0 6.8 %collective-permute-start.3 = (f16[136,512]{1,0:T(8,128)(2,1)S(1)}, f16[136,512]{1,0:T(8,128)(2,1)S(1)}, u32[]{:S(2)}, u32[]{:S(2)}) collective-permute-start(f16[136,512]{1,0:T(8,128)(2,1)S(1)} %convert_element_type.46), channel_id=1, source_target_pairs={{0,2},{1,3},{2,0},{3,1},{4,6},{5,7},{6,4},{7,5},{8,10},{9,11},{10,... | collective-permute-start | bytes 417800 | tf_op jit(solution)/shard_map/ppermute | solution.py:188
  19.8 5.7 %collective-permute-start.7 = (f16[136,512]{1,0:T(8,128)(2,1)S(1)}, f16[136,512]{1,0:T(8,128)(2,1)S(1)}, u32[]{:S(2)}, u32[]{:S(2)}) collective-permute-start(f16[136,512]{1,0:T(8,128)(2,1)S(1)} %convert_element_type.53), channel_id=1, source_target_pairs={{0,2},{1,3},{2,0},{3,1},{4,6},{5,7},{6,4},{7,5},{8,10},{9,11},{10,... | collective-permute-start | bytes 417800 | tf_op jit(solution)/shard_map/ppermute | solution.py:189
  21.9 9.0 %collective-permute-start.4 = (f16[136,256]{1,0:T(8,128)(2,1)S(1)}, f16[136,256]{1,0:T(8,128)(2,1)S(1)}, u32[]{:S(2)}, u32[]{:S(2)}) collective-permute-start(f16[136,256]{1,0:T(8,128)(2,1)S(1)} %get-tuple-element.17), channel_id=1, source_target_pairs={{0,0},{1,5},{2,2},{3,7},{4,4},{5,1},{6,6},{7,3},{8,8},{9,13},{10,1... | collective-permute-start | bytes 208904 | tf_op jit(solution)/shard_map/ppermute | solution.py:195
  25.4 5.5 %collective-permute-start.5 = (f16[136,256]{1,0:T(8,128)(2,1)S(1)}, f16[136,256]{1,0:T(8,128)(2,1)S(1)}, u32[]{:S(2)}, u32[]{:S(2)}) collective-permute-start(f16[136,256]{1,0:T(8,128)(2,1)S(1)} %get-tuple-element.18), channel_id=1, source_target_pairs={{0,1},{1,4},{2,3},{3,6},{4,5},{5,0},{6,7},{7,2},{8,9},{9,12},{10,1... | collective-permute-start | bytes 208904 | tf_op jit(solution)/shard_map/ppermute | solution.py:195
  25.5 5.3 %collective-permute-start.8 = (f16[136,256]{1,0:T(8,128)(2,1)S(1)}, f16[136,256]{1,0:T(8,128)(2,1)S(1)}, u32[]{:S(2)}, u32[]{:S(2)}) collective-permute-start(f16[136,256]{1,0:T(8,128)(2,1)S(1)} %get-tuple-element.19), channel_id=1, source_target_pairs={{0,8},{1,13},{2,10},{3,15},{4,12},{5,9},{6,14},{7,11},{8,0},{9,5},... | collective-permute-start | bytes 208904 | tf_op jit(solution)/shard_map/ppermute | solution.py:195
  27.5 8.2 %collective-permute-start.9 = (f16[136,256]{1,0:T(8,128)(2,1)S(1)}, f16[136,256]{1,0:T(8,128)(2,1)S(1)}, u32[]{:S(2)}, u32[]{:S(2)}) collective-permute-start(f16[136,256]{1,0:T(8,128)(2,1)S(1)} %get-tuple-element.20), channel_id=1, source_target_pairs={{0,9},{1,12},{2,11},{3,14},{4,13},{5,8},{6,15},{7,10},{8,1},{9,4},... | collective-permute-start | bytes 208904 | tf_op jit(solution)/shard_map/ppermute | solution.py:195

commit v4 on v2

--- a/solution.py
+++ b/solution.py
@@ -15,60 +15,95 @@
 SMEM = pl.BlockSpec(memory_space=pltpu.SMEM)
 VMEM = pl.BlockSpec(memory_space=pltpu.VMEM)
 HBM = pl.BlockSpec(memory_space=pltpu.MemorySpace.HBM)
-CHUNKS = 4
-
-
-def plan_kernel(blocks, meta, own_code, other_code, db_ref, other_ref, rows_ref, plan_ref, sems):
-    part = db_ref.shape[0] // CHUNKS
-    copies = []
-    for shard, ref in enumerate((db_ref, other_ref)):
-        for i in range(CHUNKS):
-            copies.append(pltpu.make_async_copy(
-                ref.at[pl.ds(i * part, part)],
-                rows_ref.at[pl.ds((shard * CHUNKS + i) * part, part)],
-                sems.at[shard * CHUNKS + i],
-            ))
-    for copy in copies:
-        copy.start()
-    slots = own_code.shape[1]
+GROUP = 8
+
+
+def fetch_kernel(meta, own_code, other_code, mine_ref, own_ref, other_ref, rows_ref, cut_ref, plan_ref, seen, sems, cut_sem):
+    cut = cut_ref.shape[1]
+    start = pl.multiple_of((2 * meta[2] + meta[3]) * cut, cut)
+    trim = pltpu.make_async_copy(mine_ref.at[:, pl.ds(start, cut)], cut_ref, cut_sem)
+    trim.start()
+    blocks = own_ref.shape[0] // BLK
+    for i in range(2 * blocks):
+        seen[i] = 0
+    counts = [jnp.int32(0), jnp.int32(0)]
+
+    def copy(ref, at, base):
+        start = pl.multiple_of(at * BLK, BLK)
+        to = pl.multiple_of((at + base) * BLK, BLK)
+        return pltpu.make_async_copy(
+            ref.at[pl.ds(start, BLK)], rows_ref.at[pl.ds(to, BLK)], sems.at[at + base])
+
+    for code_ref, ref, base in ((own_code, own_ref, 0), (other_code, other_ref, blocks)):
+        for j in range(code_ref.shape[1]):
+            code = code_ref[0, j]
+            at, block = code & 255, code >> 8
+            hits = [(block == meta[which]).astype(jnp.int32) for which in range(2)]
+            for which in range(2):
+                plan_ref[which, counts[which]] = base + at
+                counts[which] = counts[which] + hits[which]
+
+            @pl.when((hits[0] + hits[1] > 0) & (seen[base + at] == 0))
+            def _(ref=ref, base=base, at=at):
+                seen[base + at] = 1
+                copy(ref, at, base).start()
+
     last = plan_ref.shape[1] - 1
     for which in range(2):
-        block = meta[which]
-        n = jnp.int32(0)
-        for code_ref, base in ((own_code, 0), (other_code, blocks)):
-            def step(j, n, code_ref=code_ref, base=base):
-                code = code_ref[0, j]
-                plan_ref[which, n] = base + (code & 255)
-                return n + ((code >> 8) == block).astype(jnp.int32)
-            n = lax.fori_loop(0, slots, step, n)
-        final = plan_ref[which, jnp.maximum(n - 1, 0)]
-        final = jnp.where(n > 0, final, 0)
-        for i in range(8):
+        n = counts[which]
+        final = jnp.where(n > 0, plan_ref[which, jnp.maximum(n - 1, 0)], 0)
+        for i in range(GROUP):
             plan_ref[which, n + i] = final
         plan_ref[which, last] = n
-    for copy in copies:
-        copy.wait()
-
-
-def make_plan(meta, own_code, other_code, db, other):
+    for i in range(2 * blocks):
+        @pl.when(seen[i] == 1)
+        def _(i=i):
+            copy(own_ref, 0, i).wait()
+    trim.wait()
+
+
+def fetch(meta, own_code, other_code, mine, own, other):
+    width = own.shape[1]
+    blocks = own.shape[0] // BLK
     slots = own_code.shape[1]
     return pl.pallas_call(
-        functools.partial(plan_kernel, db.shape[0] // BLK),
+        fetch_kernel,
         out_shape=(
-            jax.ShapeDtypeStruct((2 * db.shape[0], db.shape[1]), db.dtype),
+            jax.ShapeDtypeStruct((2 * own.shape[0], width), own.dtype),
+            jax.ShapeDtypeStruct((BLK, width // 4), own.dtype),
             jax.ShapeDtypeStruct((2, 2 * slots + 16), jnp.int32),
         ),
-        in_specs=[SMEM, SMEM, SMEM, HBM, HBM],
-        out_specs=(VMEM, SMEM),
-        scratch_shapes=[pltpu.SemaphoreType.DMA((2 * CHUNKS,))],
-        compiler_params=pltpu.CompilerParams(vmem_limit_bytes=24 * 1024 * 1024),
-        name="plan",
-    )(meta, own_code, other_code, db, other)
-
-
-def block_kernel(scale, which, meta, plan, q_ref, rows_ref, send_ref, keep_ref, acc, wacc):
+        in_specs=[SMEM, SMEM, SMEM, HBM, HBM, HBM],
+        out_specs=(VMEM, VMEM, SMEM),
+        scratch_shapes=[
+            pltpu.SMEM((2 * blocks,), jnp.int32),
+            pltpu.SemaphoreType.DMA((2 * blocks,)),
+            pltpu.SemaphoreType.DMA,
+        ],
+        compiler_params=pltpu.CompilerParams(vmem_limit_bytes=12 * 1024 * 1024),
+        name="fetch",
+    )(meta, own_code, other_code, mine, own, other)
+
+
+def block_kernel(scale, which, meta, plan, q_ref, rows_ref, *refs):
     side, core = meta[2], meta[3]
     n = plan[which, plan.shape[1] - 1]
+    half_group = GROUP // 2
+    if which == 0:
+        mine_ref, send_ref, keep_ref, acc, wacc, whole, sem = refs
+        bring = pltpu.make_async_copy(mine_ref, whole, sem)
+
+        @pl.when(core == 0)
+        def _():
+            bring.start()
+            bring.wait()
+
+        @pl.when(core == 1)
+        def _():
+            whole[...] = q_ref[...]
+        q_ref = whole
+    else:
+        send_ref, keep_ref, acc, wacc = refs
     acc[...] = jnp.zeros_like(acc)
     wacc[...] = jnp.zeros_like(wacc)
 
@@ -88,17 +123,17 @@
         wacc[...] = wsum
         acc[...] += jnp.dot(w.astype(jnp.bfloat16), tile, preferred_element_type=jnp.float32)
 
-    wide = (n + 3) // 8
+    wide = (n + half_group - 1) // GROUP
 
     def step(i, carry):
-        visit(8 * i, 8)
+        visit(GROUP * i, GROUP)
         return carry
 
     lax.fori_loop(0, wide, step, 0)
 
-    @pl.when(8 * wide < n)
+    @pl.when(GROUP * wide < n)
     def _():
-        visit(8 * wide, 4)
+        visit(GROUP * wide, half_group)
 
     half = send_ref.shape[1]
     piece = half // 2
@@ -112,23 +147,22 @@
             ref[pl.ds(BLK, EXTRA), pl.ds(p * piece, piece)] = totals
 
 
-def block_sums(which, meta, plan, q, rows, scale):
+def block_sums(which, meta, plan, q, rows, *mine):
     width = q.shape[1]
+    scale = score_gain / math.sqrt(width)
     half = jax.ShapeDtypeStruct((BLK + EXTRA, width // 2), jnp.float32)
+    scratch = [pltpu.VMEM((BLK, width), jnp.float32), pltpu.VMEM((BLK, BLK), jnp.float32)]
+    if mine:
+        scratch += [pltpu.VMEM((BLK, width), q.dtype), pltpu.SemaphoreType.DMA]
     return pl.pallas_call(
         functools.partial(block_kernel, scale, which),
         out_shape=(half, half),
-        in_specs=[SMEM, SMEM, VMEM, VMEM],
+        in_specs=[SMEM, SMEM, VMEM, VMEM] + [HBM] * len(mine),
         out_specs=(VMEM, VMEM),
-        scratch_shapes=[
-            pltpu.VMEM((BLK, width), jnp.float32),
-            pltpu.VMEM((BLK, BLK), jnp.float32),
-        ],
-        compiler_params=pltpu.CompilerParams(vmem_limit_bytes=24 * 1024 * 1024),
-        cost_estimate=pl.CostEstimate(
-            flops=2 * 2 * BLK * 2048 * width, bytes_accessed=1024 * 1024, transcendentals=BLK * 2048),
+        scratch_shapes=scratch,
+        compiler_params=pltpu.CompilerParams(vmem_limit_bytes=16 * 1024 * 1024),
         name=f"block{which}",
-    )(meta, plan, q, rows)
+    )(meta, plan, q, rows, *mine)
 
 
 def paired(queries, database, pair_query, pair_db, pair_count):
@@ -136,7 +170,6 @@
     z = lax.axis_index("db")
     place = lax.axis_index("loop")
     side, core = place // 2, place % 2
-    scale = score_gain / math.sqrt(width)
     both = ("db", "loop")
     grid = [(i, j) for i in range(4) for j in range(4)]
     core_swap = [(j, j ^ 1) for j in range(4)]
@@ -147,30 +180,40 @@
 
     slot = lax.broadcasted_iota(jnp.int32, pair_query.shape, 1)
     code = jnp.where(slot < pair_count[0], pair_query * 256 + pair_db, -256)
+    other_code = lax.ppermute(code, "loop", core_swap)
     other = lax.ppermute(database, "loop", core_swap)
     second = lax.ppermute(queries, both, hop(2, 0))
-    first = lax.ppermute(queries, both, hop(0, 0))
-    other_code = lax.ppermute(code, "loop", core_swap)
+    first = lax.ppermute(queries, both, [pair for pair in hop(0, 0) if pair[0] & 1])
     meta = jnp.stack([z ^ core, z ^ core ^ 2, side, core]).astype(jnp.int32)
-    rows, plan = make_plan(meta, code, other_code, database, other)
-
-    send1, keep1 = block_sums(0, meta, plan, first, rows, scale)
-    send2, keep2 = block_sums(1, meta, plan, second, rows, scale)
+    away = pltpu.MemorySpace.HBM
+    mine = pltpu.with_memory_space_constraint(queries, away)
+    rows, own, plan = fetch(
+        meta, code, other_code, mine,
+        pltpu.with_memory_space_constraint(database, away),
+        pltpu.with_memory_space_constraint(other, away))
+    send1, keep1 = block_sums(0, meta, plan, first, rows, mine)
+    send2, keep2 = block_sums(1, meta, plan, second, rows)
+    piece = width // 4
     got1 = lax.ppermute(send1.astype(WIRE), "loop", side_swap)
     got2 = lax.ppermute(send2.astype(WIRE), "loop", side_swap)
-    sum2 = (keep2 + got2.astype(jnp.float32)).astype(WIRE)
-    sum1 = (keep1 + got1.astype(jnp.float32)).astype(WIRE)
     piece = width // 4
+
+    def pieces(keep, got):
+        return [
+            (keep[:, t * piece:(t + 1) * piece] + got[:, t * piece:(t + 1) * piece].astype(jnp.float32)).astype(WIRE)
+            for t in range(2)
+        ]
+
+    far, near = pieces(keep2, got2), pieces(keep1, got1)
     parts = [
-        lax.ppermute(sum2[:, :piece], both, hop(2, 0)),
-        lax.ppermute(sum2[:, piece:], both, hop(2, 1)),
-        lax.ppermute(sum1[:, :piece], both, hop(0, 0)),
-        lax.ppermute(sum1[:, piece:], both, hop(0, 1)),
+        lax.ppermute(far[0], both, hop(2, 0)),
+        lax.ppermute(far[1], both, hop(2, 1)),
+        jnp.where(core == 0, near[0], lax.ppermute(near[0], both, [pair for pair in hop(0, 0) if pair[0] & 1])),
+        lax.ppermute(near[1], both, hop(0, 1)),
     ]
     parts = [p.astype(jnp.float32) for p in parts]
     total = (parts[2] + parts[3]) + (parts[0] + parts[1])
-    own = lax.dynamic_slice_in_dim(queries, place * piece, piece, 1).astype(jnp.float32)
-    return own + total[:BLK] * lax.rsqrt(1.0 + total[BLK, :BLK])[:, None]
+    return own.astype(jnp.float32) + total[:BLK] * lax.rsqrt(1.0 + total[BLK, :BLK])[:, None]
 
 
 def per_device(queries, database, pair_query, pair_db, pair_count):

time: 39.3 us -> 36.4 us (0.926)
  starting transfers between devices: 15 us -> 17.5 us
  local copies, waits for them, and re-layouts: 2.24 us -> 0 us
  waiting for transfers between devices: 8.56 us -> 6.91 us
  other arithmetic: 2.53 us -> 1.7 us
    ppermute x5, starting transfers between devices: 11.3 us -> 13.6 us  [the longest x1 4.64 us: paired(): lax.ppermute(queries, both, [pair for pair in hop(0, 0) if pair[0] & 1])]
    unnamed x2 -> x0, local copies, waits for them, and re-layouts: 2.19 us -> none
    add x1, other arithmetic: 1.59 us -> 0.74 us  [paired(): own.astype(jnp.float32)]
    ppermute x5, waiting for transfers between devices: 5.66 us -> 4.82 us  [the longest x1 4.81 us: paired(): lax.ppermute(far[1], both, hop(2, 1))]
    pallas_call x2, Pallas kernels: 6.05 us -> 5.3 us  [block_sums(): pl.pallas_call(functools.partial(block_kernel, scale, which), out_shape=(...]
    ppermute x1, waiting for transfers between devices: 1.15 us -> 0.63 us  [paired(): got2 = lax.ppermute(send2.astype(WIRE), 'loop', side_swap)]
    ppermute x1, starting transfers between devices: 0.07 us -> 0.58 us  [paired(): got2 = lax.ppermute(send2.astype(WIRE), 'loop', side_swap)]
  transfers between devices with their start and end apart: 10 -> 10, of which waited for: 5 -> 4; matrix products, arithmetic and copies ran while one was open for 2% -> 2% of each run, Pallas kernels for 25% -> 26%
where the time goes in v4:
time: 36.4 us; the launch traced here: 36.2 us
  starting transfers between devices  17.5 us (48%)
  Pallas kernels  9.35 us (26%)
  waiting for transfers between devices  6.91 us (19%)
  other arithmetic  1.7 us (5%)
  between operations  0.75 us (2%)
    pallas_call x2, Pallas kernels, block_sums(): pl.pallas_call(functools.partial(block_kernel, scale, which), out_shape=(...  5.3 us
    ppermute x1, waiting for transfers between devices, paired(): lax.ppermute(far[1], both, hop(2, 1))  4.81 us
    ppermute x1, starting transfers between devices, paired(): lax.ppermute(queries, both, [pair for pair in hop(0, 0) if pair[0] & 1])  4.64 us
    ppermute x1, starting transfers between devices, paired(): lax.ppermute(far[0], both, hop(2, 0))  4.13 us
    pallas_call x1, Pallas kernels, fetch(): pl.pallas_call(fetch_kernel, out_shape=(jax.ShapeDtypeStruct((2 * own.sha...  4.05 us
    ppermute x1, starting transfers between devices, paired(): lax.ppermute(near[0], both, [pair for pair in hop(0, 0) if pair[0] & 1])  2.55 us
    ppermute x1, starting transfers between devices, paired(): second = lax.ppermute(queries, both, hop(2, 0))  2.26 us
    ppermute x1, starting transfers between devices, paired(): lax.ppermute(far[1], both, hop(2, 1))  2.19 us
  transfers between devices with their start and end apart: 10, of which 4 were waited for; matrix products, arithmetic and copies ran while one was open for 2% of the time, Pallas kernels for 26%

profile of v4, /device:TPU:1, one launch (start us, length us, event | category | flops | bytes accessed | tf_op | source)
XLA Modules:
  0.0 36.2 jit_solution(1166722394626878327)
XLA Ops:
  0.0 0.1 collective-permute-start.1
  0.1 4.6 %collective-permute-start.2 = (bf16[128,1024]{1,0:T(8,128)(2,1)}, bf16[128,1024]{1,0:T(8,128)(2,1)S(1)}, u32[]{:S(2)}, u32[]{:S(2)}) collective-permute-start(bf16[128,1024]{1,0:T(8,128)(2,1)} %refs_0_.1), channel_id=1, source_target_pairs={{1,5},{3,7},{5,1},{7,3},{9,13},{11,15},{13,9},{15,11},{17,21},{19,... | collective-permute-start | bytes 786440 | tf_op jit(solution)/shard_map/ppermute | solution.py:186
  4.7 2.3 %collective-permute-start.6 = (bf16[128,1024]{1,0:T(8,128)(2,1)}, bf16[128,1024]{1,0:T(8,128)(2,1)S(1)}, u32[]{:S(2)}, u32[]{:S(2)}) collective-permute-start(bf16[128,1024]{1,0:T(8,128)(2,1)} %refs_0_.1), channel_id=1, source_target_pairs={{0,8},{1,13},{2,10},{3,15},{4,12},{5,9},{6,14},{7,11},{8,0},{9,5},... | collective-permute-start | bytes 786440 | tf_op jit(solution)/shard_map/ppermute | solution.py:185
  7.6 0.7 %compare_select_fusion.own_code = s32[1,32]{1,0:T(1,128)S(1)} fusion(s32[1,32]{1,0:T(1,128)} %param.8, s32[1,32]{1,0:T(1,128)} %param.7, s32[]{:T(128)} %bitcast.7), kind=kLoop, calls=%fused_computation.7 | loop fusion | flops 128 | bytes 388 | tf_op jit(solution)/shard_map/jit(_where)/select_n | solution.py:182
  8.3 0.0 collective-permute-start
  8.3 0.1 pad_add_fusion.meta
  8.4 1.0 %collective-permute-done.other_code = s32[1,32]{1,0:T(1,128)S(1)} collective-permute-done((s32[1,32]{1,0:T(1,128)S(1)}, s32[1,32]{1,0:T(1,128)S(1)}, u32[]{:S(2)}, u32[]{:S(2)}) %collective-permute-start) | collective-permute-done | bytes 160 | tf_op jit(solution)/shard_map/ppermute | solution.py:183
  9.4 0.0 collective-permute-done.1.other_ref
  9.4 4.0 %fetch.1 = (bf16[4096,1024]{1,0:T(8,128)(2,1)S(1)}, bf16[128,256]{1,0:T(8,128)(2,1)S(1)}, s32[2,80]{1,0:T(2,128)S(1)}) custom-call(s32[4]{0:T(128)S(1)} %pad_add_fusion.meta, s32[1,32]{1,0:T(1,128)S(1)} %compare_select_fusion.own_code, s32[1,32]{1,0:T(1,128)S(1)} %collective-permute-done.other_code, bf16[128,1024]{1,0:T(8,128)(2,1)} %refs_0_.1, ...), custom_call_target="tpu_custom_call" | custom-call | tf_op jit(solution)/shard_map/fetch/pallas_call | solution.py:69
  13.5 0.0 collective-permute-done.2.q_ref
  13.5 2.7 %block0.1 = (f32[136,512]{1,0:T(8,128)S(1)}, f32[136,512]{1,0:T(8,128)S(1)}) custom-call(s32[4]{0:T(128)S(1)} %pad_add_fusion.meta, s32[2,80]{1,0:T(2,128)S(1)} %get-tuple-element.13.plan, bf16[128,1024]{1,0:T(8,128)(2,1)S(1)} %collective-permute-done.2.q_ref, bf16[4096,1024]{1,0:T(8,128)(2,1)S(1)} %get-tuple-element.14.rows_ref, bf16[128,1024]{1,0:T(8,128)(2,1)} %refs_0_.1), custom_call_target="tpu_custom_call" | custom-call | tf_op jit(solution)/shard_map/block0/pallas_call | solution.py:157
  16.2 1.0 %collective-permute-start.3 = (f16[136,512]{1,0:T(8,128)(2,1)S(1)}, f16[136,512]{1,0:T(8,128)(2,1)S(1)}, u32[]{:S(2)}, u32[]{:S(2)}) collective-permute-start(f16[136,512]{1,0:T(8,128)(2,1)S(1)} %convert_element_type.46), channel_id=1, source_target_pairs={{0,2},{1,3},{2,0},{3,1},{4,6},{5,7},{6,4},{7,5},{8,10},{9,11},{10,... | collective-permute-start | bytes 417800 | tf_op jit(solution)/shard_map/ppermute | solution.py:197
  17.2 0.0 collective-permute-done.6.q_ref
  17.2 2.6 %block1.1 = (f32[136,512]{1,0:T(8,128)S(1)}, f32[136,512]{1,0:T(8,128)S(1)}) custom-call(s32[4]{0:T(128)S(1)} %pad_add_fusion.meta, s32[2,80]{1,0:T(2,128)S(1)} %get-tuple-element.13.plan, bf16[128,1024]{1,0:T(8,128)(2,1)S(1)} %collective-permute-done.6.q_ref, bf16[4096,1024]{1,0:T(8,128)(2,1)S(1)} %get-tuple-element.14.rows_ref), custom_call_target="tpu_custom_call" | custom-call | tf_op jit(solution)/shard_map/block1/pallas_call | solution.py:157
  19.9 0.6 %collective-permute-start.7 = (f16[136,512]{1,0:T(8,128)(2,1)S(1)}, f16[136,512]{1,0:T(8,128)(2,1)S(1)}, u32[]{:S(2)}, u32[]{:S(2)}) collective-permute-start(f16[136,512]{1,0:T(8,128)(2,1)S(1)} %convert_element_type.53), channel_id=1, source_target_pairs={{0,2},{1,3},{2,0},{3,1},{4,6},{5,7},{6,4},{7,5},{8,10},{9,11},{10,... | collective-permute-start | bytes 417800 | tf_op jit(solution)/shard_map/ppermute | solution.py:198
  20.5 0.4 %collective-permute-done.3 = f16[136,512]{1,0:T(8,128)(2,1)S(1)} collective-permute-done((f16[136,512]{1,0:T(8,128)(2,1)S(1)}, f16[136,512]{1,0:T(8,128)(2,1)S(1)}, u32[]{:S(2)}, u32[]{:S(2)}) %collective-permute-start.3) | collective-permute-done | bytes 139296 | tf_op jit(solution)/shard_map/ppermute | solution.py:197
  20.9 2.6 %collective-permute-start.4 = (f16[136,256]{1,0:T(8,128)(2,1)S(1)}, f16[136,256]{1,0:T(8,128)(2,1)S(1)}, u32[]{:S(2)}, u32[]{:S(2)}) collective-permute-start(f16[136,256]{1,0:T(8,128)(2,1)S(1)} %get-tuple-element.19), channel_id=1, source_target_pairs={{1,5},{3,7},{5,1},{7,3},{9,13},{11,15},{13,9},{15,11},{17,21},{19,... | collective-permute-start | bytes 208904 | tf_op jit(solution)/shard_map/ppermute | solution.py:211
  23.5 0.1 collective-permute-start.5
  23.5 0.6 %collective-permute-done.7 = f16[136,512]{1,0:T(8,128)(2,1)S(1)} collective-permute-done((f16[136,512]{1,0:T(8,128)(2,1)S(1)}, f16[136,512]{1,0:T(8,128)(2,1)S(1)}, u32[]{:S(2)}, u32[]{:S(2)}) %collective-permute-start.7) | collective-permute-done | bytes 139296 | tf_op jit(solution)/shard_map/ppermute | solution.py:198
  24.2 4.1 %collective-permute-start.8 = (f16[136,256]{1,0:T(8,128)(2,1)S(1)}, f16[136,256]{1,0:T(8,128)(2,1)S(1)}, u32[]{:S(2)}, u32[]{:S(2)}) collective-permute-start(f16[136,256]{1,0:T(8,128)(2,1)S(1)} %get-tuple-element.21), channel_id=1, source_target_pairs={{0,8},{1,13},{2,10},{3,15},{4,12},{5,9},{6,14},{7,11},{8,0},{9,5},... | collective-permute-start | bytes 208904 | tf_op jit(solution)/shard_map/ppermute | solution.py:209
  28.4 2.2 %collective-permute-start.9 = (f16[136,256]{1,0:T(8,128)(2,1)S(1)}, f16[136,256]{1,0:T(8,128)(2,1)S(1)}, u32[]{:S(2)}, u32[]{:S(2)}) collective-permute-start(f16[136,256]{1,0:T(8,128)(2,1)S(1)} %get-tuple-element.22), channel_id=1, source_target_pairs={{0,9},{1,12},{2,11},{3,14},{4,13},{5,8},{6,15},{7,10},{8,1},{9,4},... | collective-permute-start | bytes 208904 | tf_op jit(solution)/shard_map/ppermute | solution.py:210
  30.5 0.0 collective-permute-done.4
  30.5 0.0 collective-permute-done.5
  30.6 0.0 collective-permute-done.8
  30.6 4.8 %collective-permute-done.9 = f16[136,256]{1,0:T(8,128)(2,1)S(1)} collective-permute-done((f16[136,256]{1,0:T(8,128)(2,1)S(1)}, f16[136,256]{1,0:T(8,128)(2,1)S(1)}, u32[]{:S(2)}, u32[]{:S(2)}) %collective-permute-start.9) | collective-permute-done | bytes 69664 | tf_op jit(solution)/shard_map/ppermute | solution.py:210
  35.4 0.1 add_add_fusion
  35.4 0.7 %fusion = f32[128,256]{1,0:T(8,128)} fusion(f32[136,256]{1,0:T(8,128)S(1)} %add_add_fusion, bf16[128,256]{1,0:T(8,128)(2,1)S(1)} %get-tuple-element.12, f32[128]{0:T(128)S(1)} %fusion.2), kind=kLoop, calls=%fused_computation.6 | loop fusion | flops 98304 | bytes 328192 | tf_op jit(solution)/shard_map/add | solution.py:216
  (5 shorter events, 0.1 us)
Async XLA Ops:
  0.0 9.4 %collective-permute-start.1 = (bf16[2048,1024]{1,0:T(8,128)(2,1)}, bf16[2048,1024]{1,0:T(8,128)(2,1)}, u32[]{:S(2)}, u32[]{:S(2)}) collective-permute-start(bf16[2048,1024]{1,0:T(8,128)(2,1)} %own_ref.1), channel_id=1, source_target_pairs={{0,1},{1,0},{2,3},{3,2},{4,5},{5,4},{6,7},{7,6},{8,9},{9,8},{10,11... | collective-permute-start | bytes 12582920 | tf_op jit(solution)/shard_map/ppermute | solution.py:184
  0.1 13.4 %collective-permute-start.2 = (bf16[128,1024]{1,0:T(8,128)(2,1)}, bf16[128,1024]{1,0:T(8,128)(2,1)S(1)}, u32[]{:S(2)}, u32[]{:S(2)}) collective-permute-start(bf16[128,1024]{1,0:T(8,128)(2,1)} %refs_0_.1), channel_id=1, source_target_pairs={{1,5},{3,7},{5,1},{7,3},{9,13},{11,15},{13,9},{15,11},{17,21},{19,... | collective-permute-start | bytes 786440 | tf_op jit(solution)/shard_map/ppermute | solution.py:186
  4.7 12.5 %collective-permute-start.6 = (bf16[128,1024]{1,0:T(8,128)(2,1)}, bf16[128,1024]{1,0:T(8,128)(2,1)S(1)}, u32[]{:S(2)}, u32[]{:S(2)}) collective-permute-start(bf16[128,1024]{1,0:T(8,128)(2,1)} %refs_0_.1), channel_id=1, source_target_pairs={{0,8},{1,13},{2,10},{3,15},{4,12},{5,9},{6,14},{7,11},{8,0},{9,5},... | collective-permute-start | bytes 786440 | tf_op jit(solution)/shard_map/ppermute | solution.py:185
  8.3 1.1 %collective-permute-start = (s32[1,32]{1,0:T(1,128)S(1)}, s32[1,32]{1,0:T(1,128)S(1)}, u32[]{:S(2)}, u32[]{:S(2)}) collective-permute-start(s32[1,32]{1,0:T(1,128)S(1)} %compare_select_fusion.own_code), channel_id=1, source_target_pairs={{0,1},{1,0},{2,3},{3,2},{4,5},{5,4},{6,7},{7,6},{8,9},{9,8},{10,11... | collective-permute-start | bytes 392 | tf_op jit(solution)/shard_map/ppermute | solution.py:183
  16.2 4.7 %collective-permute-start.3 = (f16[136,512]{1,0:T(8,128)(2,1)S(1)}, f16[136,512]{1,0:T(8,128)(2,1)S(1)}, u32[]{:S(2)}, u32[]{:S(2)}) collective-permute-start(f16[136,512]{1,0:T(8,128)(2,1)S(1)} %convert_element_type.46), channel_id=1, source_target_pairs={{0,2},{1,3},{2,0},{3,1},{4,6},{5,7},{6,4},{7,5},{8,10},{9,11},{10,... | collective-permute-start | bytes 417800 | tf_op jit(solution)/shard_map/ppermute | solution.py:197
  19.9 4.3 %collective-permute-start.7 = (f16[136,512]{1,0:T(8,128)(2,1)S(1)}, f16[136,512]{1,0:T(8,128)(2,1)S(1)}, u32[]{:S(2)}, u32[]{:S(2)}) collective-permute-start(f16[136,512]{1,0:T(8,128)(2,1)S(1)} %convert_element_type.53), channel_id=1, source_target_pairs={{0,2},{1,3},{2,0},{3,1},{4,6},{5,7},{6,4},{7,5},{8,10},{9,11},{10,... | collective-permute-start | bytes 417800 | tf_op jit(solution)/shard_map/ppermute | solution.py:198
  20.9 9.6 %collective-permute-start.4 = (f16[136,256]{1,0:T(8,128)(2,1)S(1)}, f16[136,256]{1,0:T(8,128)(2,1)S(1)}, u32[]{:S(2)}, u32[]{:S(2)}) collective-permute-start(f16[136,256]{1,0:T(8,128)(2,1)S(1)} %get-tuple-element.19), channel_id=1, source_target_pairs={{1,5},{3,7},{5,1},{7,3},{9,13},{11,15},{13,9},{15,11},{17,21},{19,... | collective-permute-start | bytes 208904 | tf_op jit(solution)/shard_map/ppermute | solution.py:211
  23.5 7.1 %collective-permute-start.5 = (f16[136,256]{1,0:T(8,128)(2,1)S(1)}, f16[136,256]{1,0:T(8,128)(2,1)S(1)}, u32[]{:S(2)}, u32[]{:S(2)}) collective-permute-start(f16[136,256]{1,0:T(8,128)(2,1)S(1)} %get-tuple-element.20), channel_id=1, source_target_pairs={{0,1},{1,4},{2,3},{3,6},{4,5},{5,0},{6,7},{7,2},{8,9},{9,12},{10,1... | collective-permute-start | bytes 208904 | tf_op jit(solution)/shard_map/ppermute | solution.py:212
  24.2 6.3 %collective-permute-start.8 = (f16[136,256]{1,0:T(8,128)(2,1)S(1)}, f16[136,256]{1,0:T(8,128)(2,1)S(1)}, u32[]{:S(2)}, u32[]{:S(2)}) collective-permute-start(f16[136,256]{1,0:T(8,128)(2,1)S(1)} %get-tuple-element.21), channel_id=1, source_target_pairs={{0,8},{1,13},{2,10},{3,15},{4,12},{5,9},{6,14},{7,11},{8,0},{9,5},... | collective-permute-start | bytes 208904 | tf_op jit(solution)/shard_map/ppermute | solution.py:209
  28.4 7.0 %collective-permute-start.9 = (f16[136,256]{1,0:T(8,128)(2,1)S(1)}, f16[136,256]{1,0:T(8,128)(2,1)S(1)}, u32[]{:S(2)}, u32[]{:S(2)}) collective-permute-start(f16[136,256]{1,0:T(8,128)(2,1)S(1)} %get-tuple-element.22), channel_id=1, source_target_pairs={{0,9},{1,12},{2,11},{3,14},{4,13},{5,8},{6,15},{7,10},{8,1},{9,4},... | collective-permute-start | bytes 208904 | tf_op jit(solution)/shard_map/ppermute | solution.py:210

commit v5 on v4

--- a/solution.py
+++ b/solution.py
@@ -176,7 +176,7 @@
     side_swap = [(j, j ^ 2) for j in range(4)]
 
     def hop(base, turn):
-        return [(4 * i + j, 4 * (i ^ (base + (j & 1))) + (j ^ turn)) for i, j in grid]
+        return [(4 * i + j, 4 * (i ^ (3 - (j & 1) if base else j & 1)) + (j ^ turn)) for i, j in grid]
 
     slot = lax.broadcasted_iota(jnp.int32, pair_query.shape, 1)
     code = jnp.where(slot < pair_count[0], pair_query * 256 + pair_db, -256)
@@ -184,35 +184,29 @@
     other = lax.ppermute(database, "loop", core_swap)
     second = lax.ppermute(queries, both, hop(2, 0))
     first = lax.ppermute(queries, both, [pair for pair in hop(0, 0) if pair[0] & 1])
-    meta = jnp.stack([z ^ core, z ^ core ^ 2, side, core]).astype(jnp.int32)
+    meta = jnp.stack([z ^ core, z ^ (3 - core), side, core]).astype(jnp.int32)
     away = pltpu.MemorySpace.HBM
     mine = pltpu.with_memory_space_constraint(queries, away)
     rows, own, plan = fetch(
         meta, code, other_code, mine,
         pltpu.with_memory_space_constraint(database, away),
         pltpu.with_memory_space_constraint(other, away))
+    piece = width // 4
+    lanes = [slice(t * piece, (t + 1) * piece) for t in range(2)]
+    send2, keep2 = block_sums(1, meta, plan, second, rows)
+    first, send2, keep2 = lax.optimization_barrier((first, send2, keep2))
+    got2 = lax.ppermute(send2.astype(WIRE), "loop", side_swap)
     send1, keep1 = block_sums(0, meta, plan, first, rows, mine)
-    send2, keep2 = block_sums(1, meta, plan, second, rows)
-    piece = width // 4
+    far = [(keep2[:, a] + got2[:, a].astype(jnp.float32)).astype(WIRE) for a in lanes]
+    send1, keep1, far = lax.optimization_barrier((send1, keep1, far))
     got1 = lax.ppermute(send1.astype(WIRE), "loop", side_swap)
-    got2 = lax.ppermute(send2.astype(WIRE), "loop", side_swap)
-    piece = width // 4
-
-    def pieces(keep, got):
-        return [
-            (keep[:, t * piece:(t + 1) * piece] + got[:, t * piece:(t + 1) * piece].astype(jnp.float32)).astype(WIRE)
-            for t in range(2)
-        ]
-
-    far, near = pieces(keep2, got2), pieces(keep1, got1)
-    parts = [
-        lax.ppermute(far[0], both, hop(2, 0)),
-        lax.ppermute(far[1], both, hop(2, 1)),
-        jnp.where(core == 0, near[0], lax.ppermute(near[0], both, [pair for pair in hop(0, 0) if pair[0] & 1])),
-        lax.ppermute(near[1], both, hop(0, 1)),
-    ]
+    near = [(keep1[:, a] + got1[:, a].astype(jnp.float32)).astype(WIRE) for a in lanes]
+    only = [pair for pair in hop(0, 0) if pair[0] & 1]
+    parts = [lax.ppermute(far[t], both, hop(2, t)) for t in range(2)]
+    parts.append(jnp.where(core == 0, near[0], lax.ppermute(near[0], both, only)))
+    parts += [lax.ppermute(near[t], both, hop(0, t)) for t in range(1, len(near))]
     parts = [p.astype(jnp.float32) for p in parts]
-    total = (parts[2] + parts[3]) + (parts[0] + parts[1])
+    total = sum(parts[2:]) + (parts[0] + parts[1])
     return own.astype(jnp.float32) + total[:BLK] * lax.rsqrt(1.0 + total[BLK, :BLK])[:, None]
 
 

time: 36.4 us -> 36.6 us (level)
  the two profiles are of different devices: /device:TPU:1 before, /device:TPU:0 now
where the time goes in v5:
time: 36.6 us; the launch traced here: 36.2 us
  starting transfers between devices  17.8 us (49%)
  Pallas kernels  10.6 us (29%)
  waiting for transfers between devices  5.32 us (15%)
  other arithmetic  1.71 us (5%)
  between operations  0.75 us (2%)
    pallas_call x2, Pallas kernels, block_sums(): pl.pallas_call(functools.partial(block_kernel, scale, which), out_shape=(...  6.63 us
    ppermute x2, starting transfers between devices, paired(): parts = [lax.ppermute(far[t], both, hop(2, t)) for t in range(2)]  4.62 us
    ppermute x1, starting transfers between devices, paired(): second = lax.ppermute(queries, both, hop(2, 0))  4.6 us
    pallas_call x1, Pallas kernels, fetch(): pl.pallas_call(fetch_kernel, out_shape=(jax.ShapeDtypeStruct((2 * own.sha...  3.98 us
    ppermute x1, starting transfers between devices, paired(): got2 = lax.ppermute(send2.astype(WIRE), 'loop', side_swap)  2.06 us
    ppermute x2, waiting for transfers between devices, paired(): parts = [lax.ppermute(far[t], both, hop(2, t)) for t in range(2)]  2.05 us
    ppermute x1, waiting for transfers between devices, paired(): lax.ppermute(near[t], both, hop(0, t))  1.95 us
    ppermute x1, starting transfers between devices, paired(): lax.ppermute(near[t], both, hop(0, t))  1.88 us
  transfers between devices with their start and end apart: 10, of which 4 were waited for; matrix products, arithmetic and copies ran while one was open for 2% of the time, Pallas kernels for 29%

profile of v5, /device:TPU:0, one launch (start us, length us, event | category | flops | bytes accessed | tf_op | source)
XLA Modules:
  0.0 36.2 jit_solution(746082512157737881)
XLA Ops:
  0.0 0.5 %collective-permute-start.1 = (bf16[2048,1024]{1,0:T(8,128)(2,1)}, bf16[2048,1024]{1,0:T(8,128)(2,1)}, u32[]{:S(2)}, u32[]{:S(2)}) collective-permute-start(bf16[2048,1024]{1,0:T(8,128)(2,1)} %own_ref.1), channel_id=1, source_target_pairs={{0,1},{1,0},{2,3},{3,2},{4,5},{5,4},{6,7},{7,6},{8,9},{9,8},{10,11... | collective-permute-start | bytes 12582920 | tf_op jit(solution)/shard_map/ppermute | solution.py:184
  0.5 4.6 %collective-permute-start.3 = (bf16[128,1024]{1,0:T(8,128)(2,1)}, bf16[128,1024]{1,0:T(8,128)(2,1)S(1)}, u32[]{:S(2)}, u32[]{:S(2)}) collective-permute-start(bf16[128,1024]{1,0:T(8,128)(2,1)} %refs_0_.1), channel_id=1, source_target_pairs={{0,12},{1,9},{2,14},{3,11},{4,8},{5,13},{6,10},{7,15},{8,4},{9,1},... | collective-permute-start | bytes 786440 | tf_op jit(solution)/shard_map/ppermute | solution.py:185
  5.1 0.7 %collective-permute-start.2 = (bf16[128,1024]{1,0:T(8,128)(2,1)}, bf16[128,1024]{1,0:T(8,128)(2,1)S(1)}, u32[]{:S(2)}, u32[]{:S(2)}) collective-permute-start(bf16[128,1024]{1,0:T(8,128)(2,1)} %refs_0_.1), channel_id=1, source_target_pairs={{1,5},{3,7},{5,1},{7,3},{9,13},{11,15},{13,9},{15,11},{17,21},{19,... | collective-permute-start | bytes 786440 | tf_op jit(solution)/shard_map/ppermute | solution.py:186
  6.4 0.7 %compare_select_fusion.own_code = s32[1,32]{1,0:T(1,128)S(1)} fusion(s32[1,32]{1,0:T(1,128)} %param.8, s32[1,32]{1,0:T(1,128)} %param.7, s32[]{:T(128)} %bitcast.7), kind=kLoop, calls=%fused_computation.7 | loop fusion | flops 128 | bytes 388 | tf_op jit(solution)/shard_map/jit(_where)/select_n | solution.py:182
  7.0 1.7 %collective-permute-start = (s32[1,32]{1,0:T(1,128)S(1)}, s32[1,32]{1,0:T(1,128)S(1)}, u32[]{:S(2)}, u32[]{:S(2)}) collective-permute-start(s32[1,32]{1,0:T(1,128)S(1)} %compare_select_fusion.own_code), channel_id=1, source_target_pairs={{0,1},{1,0},{2,3},{3,2},{4,5},{5,4},{6,7},{7,6},{8,9},{9,8},{10,11... | collective-permute-start | bytes 392 | tf_op jit(solution)/shard_map/ppermute | solution.py:183
  8.8 0.1 pad_add_fusion.meta
  8.9 0.7 %collective-permute-done.other_code = s32[1,32]{1,0:T(1,128)S(1)} collective-permute-done((s32[1,32]{1,0:T(1,128)S(1)}, s32[1,32]{1,0:T(1,128)S(1)}, u32[]{:S(2)}, u32[]{:S(2)}) %collective-permute-start) | collective-permute-done | bytes 160 | tf_op jit(solution)/shard_map/ppermute | solution.py:183
  9.6 0.0 collective-permute-done.1.other_ref
  9.6 4.0 %fetch.1 = (bf16[4096,1024]{1,0:T(8,128)(2,1)S(1)}, bf16[128,256]{1,0:T(8,128)(2,1)S(1)}, s32[2,80]{1,0:T(2,128)S(1)}) custom-call(s32[4]{0:T(128)S(1)} %pad_add_fusion.meta, s32[1,32]{1,0:T(1,128)S(1)} %compare_select_fusion.own_code, s32[1,32]{1,0:T(1,128)S(1)} %collective-permute-done.other_code, bf16[128,1024]{1,0:T(8,128)(2,1)} %refs_0_.1, ...), custom_call_target="tpu_custom_call" | custom-call | tf_op jit(solution)/shard_map/fetch/pallas_call | solution.py:69
  13.6 0.0 collective-permute-done.3.q_ref
  13.6 2.6 %block1.1 = (f32[136,512]{1,0:T(8,128)S(1)}, f32[136,512]{1,0:T(8,128)S(1)}) custom-call(s32[4]{0:T(128)S(1)} %pad_add_fusion.meta, s32[2,80]{1,0:T(2,128)S(1)} %get-tuple-element.20.plan, bf16[128,1024]{1,0:T(8,128)(2,1)S(1)} %collective-permute-done.3.q_ref, bf16[4096,1024]{1,0:T(8,128)(2,1)S(1)} %get-tuple-element.21.rows_ref), custom_call_target="tpu_custom_call" | custom-call | tf_op jit(solution)/shard_map/block1/pallas_call | solution.py:157
  16.2 0.0 collective-permute-done.2.q_ref
  16.3 2.1 %collective-permute-start.4 = (f16[136,512]{1,0:T(8,128)(2,1)S(1)}, f16[136,512]{1,0:T(8,128)(2,1)S(1)}, u32[]{:S(2)}, u32[]{:S(2)}) collective-permute-start(f16[136,512]{1,0:T(8,128)(2,1)S(1)} %convert_element_type.46), channel_id=1, source_target_pairs={{0,2},{1,3},{2,0},{3,1},{4,6},{5,7},{6,4},{7,5},{8,10},{9,11},{10,... | collective-permute-start | bytes 417800 | tf_op jit(solution)/shard_map/ppermute | solution.py:198
  18.3 4.0 %block0.1 = (f32[136,512]{1,0:T(8,128)S(1)}, f32[136,512]{1,0:T(8,128)S(1)}) custom-call(s32[4]{0:T(128)S(1)} %pad_add_fusion.meta, s32[2,80]{1,0:T(2,128)S(1)} %get-tuple-element.20.plan, bf16[128,1024]{1,0:T(8,128)(2,1)S(1)} %collective-permute-done.2.q_ref, bf16[4096,1024]{1,0:T(8,128)(2,1)S(1)} %get-tuple-element.21.rows_ref, bf16[128,1024]{1,0:T(8,128)(2,1)} %refs_0_.1), custom_call_target="tpu_custom_call" | custom-call | tf_op jit(solution)/shard_map/block0/pallas_call | solution.py:157
  22.4 0.0 collective-permute-done.4
  22.4 0.1 add_convert_fusion.2
  22.4 1.1 %collective-permute-start.5 = (f16[136,512]{1,0:T(8,128)(2,1)S(1)}, f16[136,512]{1,0:T(8,128)(2,1)S(1)}, u32[]{:S(2)}, u32[]{:S(2)}) collective-permute-start(f16[136,512]{1,0:T(8,128)(2,1)S(1)} %convert_element_type.51), channel_id=1, source_target_pairs={{0,2},{1,3},{2,0},{3,1},{4,6},{5,7},{6,4},{7,5},{8,10},{9,11},{10,... | collective-permute-start | bytes 417800 | tf_op jit(solution)/shard_map/ppermute | solution.py:202
  23.5 3.4 %collective-permute-start.8 = (f16[136,256]{1,0:T(8,128)(2,1)S(1)}, f16[136,256]{1,0:T(8,128)(2,1)S(1)}, u32[]{:S(2)}, u32[]{:S(2)}) collective-permute-start(f16[136,256]{1,0:T(8,128)(2,1)S(1)} %get-tuple-element.31), channel_id=1, source_target_pairs={{0,12},{1,9},{2,14},{3,11},{4,8},{5,13},{6,10},{7,15},{8,4},{9,1},... | collective-permute-start | bytes 208904 | tf_op jit(solution)/shard_map/ppermute | solution.py:205
  26.9 1.2 %collective-permute-start.9 = (f16[136,256]{1,0:T(8,128)(2,1)S(1)}, f16[136,256]{1,0:T(8,128)(2,1)S(1)}, u32[]{:S(2)}, u32[]{:S(2)}) collective-permute-start(f16[136,256]{1,0:T(8,128)(2,1)S(1)} %get-tuple-element.32), channel_id=1, source_target_pairs={{0,13},{1,8},{2,15},{3,10},{4,9},{5,12},{6,11},{7,14},{8,5},{9,0},... | collective-permute-start | bytes 208904 | tf_op jit(solution)/shard_map/ppermute | solution.py:205
  28.2 0.6 %collective-permute-done.5 = f16[136,512]{1,0:T(8,128)(2,1)S(1)} collective-permute-done((f16[136,512]{1,0:T(8,128)(2,1)S(1)}, f16[136,512]{1,0:T(8,128)(2,1)S(1)}, u32[]{:S(2)}, u32[]{:S(2)}) %collective-permute-start.5) | collective-permute-done | bytes 139296 | tf_op jit(solution)/shard_map/ppermute | solution.py:202
  28.8 0.7 %collective-permute-start.6 = (f16[136,256]{1,0:T(8,128)(2,1)S(1)}, f16[136,256]{1,0:T(8,128)(2,1)S(1)}, u32[]{:S(2)}, u32[]{:S(2)}) collective-permute-start(f16[136,256]{1,0:T(8,128)(2,1)S(1)} %get-tuple-element.33), channel_id=1, source_target_pairs={{1,5},{3,7},{5,1},{7,3},{9,13},{11,15},{13,9},{15,11},{17,21},{19,... | collective-permute-start | bytes 208904 | tf_op jit(solution)/shard_map/ppermute | solution.py:206
  29.5 1.9 %collective-permute-start.7 = (f16[136,256]{1,0:T(8,128)(2,1)S(1)}, f16[136,256]{1,0:T(8,128)(2,1)S(1)}, u32[]{:S(2)}, u32[]{:S(2)}) collective-permute-start(f16[136,256]{1,0:T(8,128)(2,1)S(1)} %get-tuple-element.34), channel_id=1, source_target_pairs={{0,1},{1,4},{2,3},{3,6},{4,5},{5,0},{6,7},{7,2},{8,9},{9,12},{10,1... | collective-permute-start | bytes 208904 | tf_op jit(solution)/shard_map/ppermute | solution.py:207
  31.3 0.0 collective-permute-done.8
  31.3 2.0 %collective-permute-done.9 = f16[136,256]{1,0:T(8,128)(2,1)S(1)} collective-permute-done((f16[136,256]{1,0:T(8,128)(2,1)S(1)}, f16[136,256]{1,0:T(8,128)(2,1)S(1)}, u32[]{:S(2)}, u32[]{:S(2)}) %collective-permute-start.9) | collective-permute-done | bytes 69664 | tf_op jit(solution)/shard_map/ppermute | solution.py:205
  33.4 0.0 collective-permute-done.6
  33.4 1.9 %collective-permute-done.7 = f16[136,256]{1,0:T(8,128)(2,1)S(1)} collective-permute-done((f16[136,256]{1,0:T(8,128)(2,1)S(1)}, f16[136,256]{1,0:T(8,128)(2,1)S(1)}, u32[]{:S(2)}, u32[]{:S(2)}) %collective-permute-start.7) | collective-permute-done | bytes 69664 | tf_op jit(solution)/shard_map/ppermute | solution.py:207
  35.3 0.1 add_add_fusion
  35.4 0.7 %fusion = f32[128,256]{1,0:T(8,128)} fusion(f32[136,256]{1,0:T(8,128)S(1)} %add_add_fusion, bf16[128,256]{1,0:T(8,128)(2,1)S(1)} %get-tuple-element.19, f32[128]{0:T(128)S(1)} %fusion.2), kind=kLoop, calls=%fused_computation.6 | loop fusion | flops 98304 | bytes 328192 | tf_op jit(solution)/shard_map/add | solution.py:210
  (4 shorter events, 0.1 us)
Async XLA Ops:
  0.0 9.6 %collective-permute-start.1 = (bf16[2048,1024]{1,0:T(8,128)(2,1)}, bf16[2048,1024]{1,0:T(8,128)(2,1)}, u32[]{:S(2)}, u32[]{:S(2)}) collective-permute-start(bf16[2048,1024]{1,0:T(8,128)(2,1)} %own_ref.1), channel_id=1, source_target_pairs={{0,1},{1,0},{2,3},{3,2},{4,5},{5,4},{6,7},{7,6},{8,9},{9,8},{10,11... | collective-permute-start | bytes 12582920 | tf_op jit(solution)/shard_map/ppermute | solution.py:184
  0.5 13.2 %collective-permute-start.3 = (bf16[128,1024]{1,0:T(8,128)(2,1)}, bf16[128,1024]{1,0:T(8,128)(2,1)S(1)}, u32[]{:S(2)}, u32[]{:S(2)}) collective-permute-start(bf16[128,1024]{1,0:T(8,128)(2,1)} %refs_0_.1), channel_id=1, source_target_pairs={{0,12},{1,9},{2,14},{3,11},{4,8},{5,13},{6,10},{7,15},{8,4},{9,1},... | collective-permute-start | bytes 786440 | tf_op jit(solution)/shard_map/ppermute | solution.py:185
  5.1 11.2 %collective-permute-start.2 = (bf16[128,1024]{1,0:T(8,128)(2,1)}, bf16[128,1024]{1,0:T(8,128)(2,1)S(1)}, u32[]{:S(2)}, u32[]{:S(2)}) collective-permute-start(bf16[128,1024]{1,0:T(8,128)(2,1)} %refs_0_.1), channel_id=1, source_target_pairs={{1,5},{3,7},{5,1},{7,3},{9,13},{11,15},{13,9},{15,11},{17,21},{19,... | collective-permute-start | bytes 786440 | tf_op jit(solution)/shard_map/ppermute | solution.py:186
  7.0 2.6 %collective-permute-start = (s32[1,32]{1,0:T(1,128)S(1)}, s32[1,32]{1,0:T(1,128)S(1)}, u32[]{:S(2)}, u32[]{:S(2)}) collective-permute-start(s32[1,32]{1,0:T(1,128)S(1)} %compare_select_fusion.own_code), channel_id=1, source_target_pairs={{0,1},{1,0},{2,3},{3,2},{4,5},{5,4},{6,7},{7,6},{8,9},{9,8},{10,11... | collective-permute-start | bytes 392 | tf_op jit(solution)/shard_map/ppermute | solution.py:183
  16.3 6.1 %collective-permute-start.4 = (f16[136,512]{1,0:T(8,128)(2,1)S(1)}, f16[136,512]{1,0:T(8,128)(2,1)S(1)}, u32[]{:S(2)}, u32[]{:S(2)}) collective-permute-start(f16[136,512]{1,0:T(8,128)(2,1)S(1)} %convert_element_type.46), channel_id=1, source_target_pairs={{0,2},{1,3},{2,0},{3,1},{4,6},{5,7},{6,4},{7,5},{8,10},{9,11},{10,... | collective-permute-start | bytes 417800 | tf_op jit(solution)/shard_map/ppermute | solution.py:198
  22.4 6.3 %collective-permute-start.5 = (f16[136,512]{1,0:T(8,128)(2,1)S(1)}, f16[136,512]{1,0:T(8,128)(2,1)S(1)}, u32[]{:S(2)}, u32[]{:S(2)}) collective-permute-start(f16[136,512]{1,0:T(8,128)(2,1)S(1)} %convert_element_type.51), channel_id=1, source_target_pairs={{0,2},{1,3},{2,0},{3,1},{4,6},{5,7},{6,4},{7,5},{8,10},{9,11},{10,... | collective-permute-start | bytes 417800 | tf_op jit(solution)/shard_map/ppermute | solution.py:202
  23.5 7.8 %collective-permute-start.8 = (f16[136,256]{1,0:T(8,128)(2,1)S(1)}, f16[136,256]{1,0:T(8,128)(2,1)S(1)}, u32[]{:S(2)}, u32[]{:S(2)}) collective-permute-start(f16[136,256]{1,0:T(8,128)(2,1)S(1)} %get-tuple-element.31), channel_id=1, source_target_pairs={{0,12},{1,9},{2,14},{3,11},{4,8},{5,13},{6,10},{7,15},{8,4},{9,1},... | collective-permute-start | bytes 208904 | tf_op jit(solution)/shard_map/ppermute | solution.py:205
  26.9 6.4 %collective-permute-start.9 = (f16[136,256]{1,0:T(8,128)(2,1)S(1)}, f16[136,256]{1,0:T(8,128)(2,1)S(1)}, u32[]{:S(2)}, u32[]{:S(2)}) collective-permute-start(f16[136,256]{1,0:T(8,128)(2,1)S(1)} %get-tuple-element.32), channel_id=1, source_target_pairs={{0,13},{1,8},{2,15},{3,10},{4,9},{5,12},{6,11},{7,14},{8,5},{9,0},... | collective-permute-start | bytes 208904 | tf_op jit(solution)/shard_map/ppermute | solution.py:205
  28.8 4.6 %collective-permute-start.6 = (f16[136,256]{1,0:T(8,128)(2,1)S(1)}, f16[136,256]{1,0:T(8,128)(2,1)S(1)}, u32[]{:S(2)}, u32[]{:S(2)}) collective-permute-start(f16[136,256]{1,0:T(8,128)(2,1)S(1)} %get-tuple-element.33), channel_id=1, source_target_pairs={{1,5},{3,7},{5,1},{7,3},{9,13},{11,15},{13,9},{15,11},{17,21},{19,... | collective-permute-start | bytes 208904 | tf_op jit(solution)/shard_map/ppermute | solution.py:206
  29.5 5.9 %collective-permute-start.7 = (f16[136,256]{1,0:T(8,128)(2,1)S(1)}, f16[136,256]{1,0:T(8,128)(2,1)S(1)}, u32[]{:S(2)}, u32[]{:S(2)}) collective-permute-start(f16[136,256]{1,0:T(8,128)(2,1)S(1)} %get-tuple-element.34), channel_id=1, source_target_pairs={{0,1},{1,4},{2,3},{3,6},{4,5},{5,0},{6,7},{7,2},{8,9},{9,12},{10,1... | collective-permute-start | bytes 208904 | tf_op jit(solution)/shard_map/ppermute | solution.py:207
